TPU v7x, 32 devices: a whole 2x2x4 slice. The times are simulated.
32 devices in a mesh: section: 4 (over y, x), shard: 8 (over z, core).
Axes of the slice: x: 2, y: 2, z: 4, core: 2. Of those that a mesh axis runs over, the one named last changes fastest.
Arguments:
- activations: bfloat16 [4, 768, 4096], P('section', 'shard'), may hold values from -30 to 30, as said below
- top_grad: bfloat16 [768, 4096], P('shard'), may hold values from -6 to 6
- loss_mask: int32 [768], P('shard'), may hold values 0 or 1
- norm_gain: float32 [4, 4096], P('section'), may hold values from 0.5 to 1.5
- value_weight: bfloat16 [4, 4096, 1024], P('section', 'shard'), may hold values from -0.046875 to 0.046875
- output_weight: bfloat16 [4, 1024, 4096], P('section', None, 'shard'), may hold values from -0.09375 to 0.09375
- value_proj: bfloat16 [4, 1024, 64], P('section'), may hold values from -0.1875 to 0.1875
- grad_proj: bfloat16 [4, 4096, 64], P('section'), may hold values from -0.09375 to 0.09375
- store: float32 [4, 1024, 4096], P('section', 'shard'), may hold values from -0.024 to 0.024
Outputs:
- scores: float32 [8, 1024], P('section', 'shard')
Inputs may be any that keep to these rules, and one draw needn't show every extreme that they name: activations of order one per token.
All inputs are finite; a program needn't handle non-finite values. No bound on the sum of `loss_mask` on one device may be relied on, other than what follows from the above.
Results may differ from a plain program's by a relative error of at most 0.007.
Values may be sent and summed in bfloat16 or wider, within the bound.
No kernel may reach another device: no remote copies, remote signals or barrier semaphores. Data moves between devices by JAX's collectives and lax.ppermute only.
A program may use at most 128 MiB of HBM per device.

v0:
```python
import jax
import jax.numpy as jnp
from jax import lax
from jax.sharding import PartitionSpec as P

LEN = 96


EPSILON = 1e-05


def shifted(value, axis, steps):
    count = lax.axis_size(axis)
    leading, last = (max(0, -steps), min(count, count - steps))
    return lax.ppermute(value, axis, [(source, source + steps) for source in range(leading, last)])


def per_device(
    activations,
    top_grad,
    loss_mask,
    norm_gain,
    value_weight,
    output_weight,
    value_proj,
    grad_proj,
    store,
):
    section_count = lax.axis_size("section")
    section_index = lax.axis_index("section")
    hidden_in = activations[0].astype(jnp.float32)
    norm_scale = norm_gain[0]
    inverse_rms = lax.rsqrt(jnp.mean(hidden_in * hidden_in, axis=-1, keepdims=True) + EPSILON)
    normed = (hidden_in * inverse_rms * norm_scale).astype(jnp.bfloat16)
    value_local = value_weight[0]
    output_local = output_weight[0]
    value_full, output_full = (
        lax.all_gather(value_local, "shard", axis=0, tiled=True),
        lax.all_gather(output_local, "shard", axis=1, tiled=True),
    )
    value_sum = jnp.dot(normed, value_full, preferred_element_type=jnp.float32)
    value_act = value_sum.astype(jnp.bfloat16)
    value_low = jnp.dot(value_act, value_proj[0], preferred_element_type=jnp.float32)
    cotangent_top = (top_grad.astype(jnp.float32) * loss_mask.astype(jnp.float32)[:, None]).astype(
        jnp.bfloat16
    )
    token_count = top_grad.shape[0]
    model_width = top_grad.shape[1]
    proj_width = value_proj.shape[2]
    gen_local = token_count // LEN
    blocks = 1
    block_rows = token_count // blocks
    gens_block = max(block_rows // LEN, 1)

    def descend(incoming):
        grad_value = lax.dot_general(
            incoming, output_full, (((1,), (1,)), ((), ())), preferred_element_type=jnp.float32
        ).astype(jnp.bfloat16)
        grad_normed = lax.dot_general(
            grad_value, value_full, (((1,), (1,)), ((), ())), preferred_element_type=jnp.float32
        )
        scaled = norm_scale * grad_normed
        correction = jnp.mean(scaled * hidden_in, axis=-1, keepdims=True)
        grad_input = (
            inverse_rms * scaled
            - hidden_in * (inverse_rms * inverse_rms * inverse_rms) * correction
        )
        return (incoming.astype(jnp.float32) + grad_input).astype(jnp.bfloat16)

    def active(features, incoming, block_index):
        grad_low = jnp.dot(incoming, grad_proj[0], preferred_element_type=jnp.float32)
        outer = jnp.einsum(
            "gta,gtb->gab",
            grad_low.reshape(gens_block, LEN, proj_width),
            value_low.reshape(gens_block, LEN, proj_width),
            precision=lax.Precision.HIGHEST,
        ).reshape(gens_block, proj_width * proj_width)
        features = outer
        outgoing = lax.cond(
            section_index > 0,
            lambda operand: descend(operand),
            lambda operand: jnp.zeros_like(operand),
            incoming,
        )
        return (features, outgoing)

    def resting(features, incoming, block_index):
        return (features, jnp.zeros_like(incoming))

    features = jnp.zeros((gen_local, proj_width * proj_width), jnp.float32)
    outgoing = jnp.zeros((block_rows, model_width), jnp.bfloat16)
    for section_turn in range(section_count + blocks - 1):
        if section_turn > 0:
            received = shifted(outgoing, "section", -1)
        else:
            received = jnp.zeros_like(outgoing)
        incoming = jnp.where(section_index == section_count - 1, cotangent_top, received)
        block_number = section_turn - (section_count - 1 - section_index)
        working = (block_number >= 0) & (block_number < blocks)
        block_index = jnp.clip(block_number, 0, blocks - 1)
        features, outgoing = lax.cond(working, active, resting, features, incoming, block_index)
    gathered = lax.all_gather(features, "shard", axis=0, tiled=True)
    rows_out = gathered.shape[0] // section_count
    partial_value = lax.dot_general(
        gathered,
        store[0],
        (((1,), (1,)), ((), ())),
        precision=lax.Precision.HIGHEST,
        preferred_element_type=jnp.float32,
    )
    score_total = lax.psum(partial_value, "section")
    result = lax.dynamic_slice_in_dim(score_total, section_index * rows_out, rows_out, 0)
    return result


def solution(mesh):
    placed = (
        P("section", "shard", None),
        P("shard", None),
        P("shard"),
        P("section", None),
        P("section", "shard", None),
        P("section", None, "shard"),
        P("section", None, None),
        P("section", None, None),
        P("section", "shard", None),
    )
    return jax.shard_map(
        per_device, mesh=mesh, in_specs=placed, out_specs=P("section", "shard"), check_vma=False
    )
```

profile of v0, /device:TPU:0, one launch (start us, length us, event | category | flops | bytes accessed | tf_op | source)
XLA Modules:
  0.0 327.0 jit_solution(6012886263952559852)
XLA Ops:
  6.5 0.7 all-gather.8.cloned.1.call-update
  8.3 2.3 multiply_convert_fusion.1
  10.6 1.3 bitcast_convert_fusion
  11.9 81.9 %all-gather.8.cloned.1.call-done = bf16[1,4096,1024]{2,1,0:T(8,128)(2,1)} async-done(((bf16[1,512,1024]{2,1,0:T(8,128)(2,1)}), bf16[1,4096,1024]{2,1,0:T(8,128)(2,1)}) %all-gather.8.cloned.1.call-update) | async-done | bytes 8388624 | tf_op jit(solution)/shard_map/all_gather | solution.py:38
  93.8 5.1 %fusion.15 = f32[96,64]{0,1:T(8,128)S(1)} fusion(bf16[1,96,4096]{2,1,0:T(8,128)(2,1)S(1)} %copy-done.1, f32[4096]{0:T(1024)S(1)} %bitcast.81, f32[96]{0:T(128)S(1)} %get-tuple-element.294, bf16[1,1024,64]{1,2,0:T(8,128)(2,1)} %param.29, bf16[1,4096,1024]{2,1,0:T(8,128)(2,1)} %all-gather.8.cloned.1.call-done), kind=kOutput, calls=%fused_computation.40 | convolution fusion | flops 819560448 | bytes 9347456 | tf_op jit(solution)/shard_map/dot_general | solution.py:43
  98.9 77.1 %all-gather.6.cloned.1.call-done = bf16[1,1024,4096]{2,1,0:T(8,128)(2,1)} async-done(((bf16[1,1024,512]{2,1,0:T(8,128)(2,1)}), bf16[1,1024,4096]{2,1,0:T(8,128)(2,1)}) %all-gather.6.cloned.1.call-update) | async-done | bytes 8388624 | tf_op jit(solution)/shard_map/all_gather | solution.py:39
  176.0 1.0 conditional.7
  176.0 1.0 broadcast.64
  177.0 1.3 collective-permute-start
  178.3 20.5 %collective-permute-done = bf16[96,4096]{1,0:T(8,128)(2,1)S(1)} collective-permute-done((bf16[96,4096]{1,0:T(8,128)(2,1)}, bf16[96,4096]{1,0:T(8,128)(2,1)S(1)}, u32[]{:S(2)}, u32[]{:S(2)}) %collective-permute-start) | collective-permute-done | bytes 786464 | tf_op jit(solution)/shard_map/ppermute | solution.py:15
  198.8 1.0 conditional.8
  198.8 1.0 broadcast.67
  199.7 1.5 collective-permute-start.1
  201.2 20.1 %collective-permute-done.1 = bf16[96,4096]{1,0:T(8,128)(2,1)S(1)} collective-permute-done((bf16[96,4096]{1,0:T(8,128)(2,1)}, bf16[96,4096]{1,0:T(8,128)(2,1)S(1)}, u32[]{:S(2)}, u32[]{:S(2)}) %collective-permute-start.1) | collective-permute-done | bytes 786464 | tf_op jit(solution)/shard_map/ppermute | solution.py:15
  221.3 1.0 conditional.9
  221.3 1.0 broadcast.70
  222.3 1.3 collective-permute-start.2
  223.6 70.2 %collective-permute-done.2 = bf16[96,4096]{1,0:T(8,128)(2,1)S(1)} collective-permute-done((bf16[96,4096]{1,0:T(8,128)(2,1)}, bf16[96,4096]{1,0:T(8,128)(2,1)S(1)}, u32[]{:S(2)}, u32[]{:S(2)}) %collective-permute-start.2) | collective-permute-done | bytes 786464 | tf_op jit(solution)/shard_map/ppermute | solution.py:15
  293.8 2.7 conditional.10
  293.8 0.9 copy-done.6
  294.6 1.5 fusion.7
  296.5 14.0 %all-gather.2 = f32[8,1,4096]{2,1,0:T(1,128)S(1)} all-gather(f32[1,1,4096]{2,1,0:T(1,128)S(1)} %bitcast.85), channel_id=1, replica_groups=mesh['section'=4,'shard'=8] {'shard'}, dimensions={0}, use_global_device_ids=true | all-gather | bytes 147456 | tf_op jit(solution)/shard_map/all_gather | solution.py:102
  310.4 1.7 fusion.13
  312.2 7.5 %psum.7 = f32[8,128]{1,0:T(8,128)S(1)} all-reduce(f32[8,128]{1,0:T(8,128)S(1)} %fusion.13), channel_id=1, replica_groups=mesh['section'=4,'shard'=8] {'section'}, use_global_device_ids=true, to_apply=%region_18.19 | all-reduce | flops 1024 | bytes 8192 | tf_op jit(solution)/shard_map/psum | solution.py:111
  (21 shorter events, 1.9 us)
Async XLA Ops:
  6.5 303.9 %copy-start = (f32[1,128,4096]{2,1,0:T(8,128)S(1)}, f32[1,128,4096]{2,1,0:T(8,128)}, u32[]{:S(2)}) copy-start(f32[1,128,4096]{2,1,0:T(8,128)} %param.31) | copy-start | bytes 6291460
  6.5 1.5 copy-start.7
  6.5 1.5 copy-start.1
  6.5 87.2 %all-gather.8.cloned.1.call-start = ((), (), s32[]{:S(2)}) async-start(), calls=%async_computation.1 | async-start | bytes 9437184 | tf_op jit(solution)/shard_map/all_gather | solution.py:38
  7.3 168.7 %all-gather.6.cloned.1.call-start = ((), (), s32[]{:S(2)}) async-start(), calls=%async_computation | async-start | bytes 9437184 | tf_op jit(solution)/shard_map/all_gather | solution.py:39
  10.6 83.2 %copy-start.5 = (f32[1,4096]{1,0:T(1,128)S(1)}, f32[1,4096]{1,0:T(1,128)}, u32[]{:S(2)}) copy-start(f32[1,4096]{1,0:T(1,128)} %param.26) | copy-start | bytes 49156
  93.8 82.2 %copy-start.2 = (bf16[1,4096,64]{1,2,0:T(8,128)(2,1)S(1)}, bf16[1,4096,64]{1,2,0:T(8,128)(2,1)}, u32[]{:S(2)}) copy-start(bf16[1,4096,64]{1,2,0:T(8,128)(2,1)} %param.30) | copy-start | bytes 1572868
  177.0 21.8 %collective-permute-start = (bf16[96,4096]{1,0:T(8,128)(2,1)}, bf16[96,4096]{1,0:T(8,128)(2,1)S(1)}, u32[]{:S(2)}, u32[]{:S(2)}) collective-permute-start(bf16[96,4096]{1,0:T(8,128)(2,1)} %get-tuple-element.172), channel_id=1, source_target_pairs={{8,0},{16,8},{24,16},{9,1},{17,9},{25,17},{10,2},{18,10},{26,18},{... | collective-permute-start | bytes 2359304 | tf_op jit(solution)/shard_map/ppermute | solution.py:15
  199.7 21.6 %collective-permute-start.1 = (bf16[96,4096]{1,0:T(8,128)(2,1)}, bf16[96,4096]{1,0:T(8,128)(2,1)S(1)}, u32[]{:S(2)}, u32[]{:S(2)}) collective-permute-start(bf16[96,4096]{1,0:T(8,128)(2,1)} %get-tuple-element.174), channel_id=1, source_target_pairs={{8,0},{16,8},{24,16},{9,1},{17,9},{25,17},{10,2},{18,10},{26,18},{... | collective-permute-start | bytes 2359304 | tf_op jit(solution)/shard_map/ppermute | solution.py:15
  222.3 71.5 %collective-permute-start.2 = (bf16[96,4096]{1,0:T(8,128)(2,1)}, bf16[96,4096]{1,0:T(8,128)(2,1)S(1)}, u32[]{:S(2)}, u32[]{:S(2)}) collective-permute-start(bf16[96,4096]{1,0:T(8,128)(2,1)} %get-tuple-element.176), channel_id=1, source_target_pairs={{8,0},{16,8},{24,16},{9,1},{17,9},{25,17},{10,2},{18,10},{26,18},{... | collective-permute-start | bytes 2359304 | tf_op jit(solution)/shard_map/ppermute | solution.py:15
  293.8 0.9 copy-start.6
Sparse Core Ops, SparseCore 0:
  9.0 84.7 all-gather.7
  95.4 80.5 all-gather.5
where the time goes:
time: 327 us
  waiting for transfers between devices  271 us (83%)
  blocking collectives  21.4 us (7%)
  between operations  13.5 us (4%)
  matrix products  8.57 us (3%)
  local copies, waits for them, and re-layouts  4.42 us (1%)
  starting transfers between devices  4.07 us (1%)
  other arithmetic  3.83 us (1%)
    ppermute x3, waiting for transfers between devices, shifted(): lax.ppermute(value, axis, [(source, source + steps) for source in range(l...  111 us
    all_gather x1, waiting for transfers between devices, per_device(): lax.all_gather(value_local, 'shard', axis=0, tiled=True)  81.9 us
    all_gather x1, waiting for transfers between devices, per_device(): lax.all_gather(output_local, 'shard', axis=1, tiled=True)  77.1 us
    all_gather x1, blocking collectives, per_device(): gathered = lax.all_gather(features, 'shard', axis=0, tiled=True)  14 us
    psum x1, blocking collectives, per_device(): score_total = lax.psum(partial_value, 'section')  7.46 us
  transfers between devices with their start and end apart: 5, of which 5 were waited for; matrix products, arithmetic and copies ran while one was open for 3% of the time, Pallas kernels for 0%

commit v1 on v0

v1 whole, which is shorter than its diff:
```python
import jax
import jax.numpy as jnp
from jax import lax
from jax.sharding import PartitionSpec as P

LEN = 96
EPSILON = 1e-05
BF16 = jnp.bfloat16
F32 = jnp.float32


def swap(value, axis, step):
    return lax.ppermute(value, axis, [(i, i ^ step) for i in range(lax.axis_size(axis))])


def spread(rows):
    count = lax.axis_size("shard")
    index = lax.axis_index("shard")
    half = count // 2
    width = rows.shape[1] // count

    def piece(step):
        return lax.dynamic_slice_in_dim(rows, (index ^ step) * width, width, 1)

    keep = jnp.stack([piece(2 * z) for z in range(half)])
    away = jnp.stack([piece(2 * z + 1) for z in range(half)])
    both = [keep, swap(away, "shard", 1)]
    got = [jnp.stack([part[0] for part in both])]
    for z in range(1, half):
        got.append(swap(jnp.stack([part[z] for part in both]), "shard", 2 * z))
    return jnp.stack(got, axis=1)


def scatter_sum(parts):
    half = parts.shape[1]
    pair = (parts[0].astype(F32) + swap(parts[1], "shard", 1).astype(F32)).astype(parts.dtype)
    total = pair[0].astype(F32)
    for z in range(1, half):
        total = total + swap(pair[z], "shard", 2 * z).astype(F32)
    return total


def gather_rows(rows):
    half = lax.axis_size("shard") // 2
    column = jnp.stack([rows] + [swap(rows, "shard", 2 * z) for z in range(1, half)])
    return jnp.stack([column, swap(column, "shard", 1)])


def exchange(value):
    count = lax.axis_size("section")
    out = [value]
    for step in range(1, count):
        pairs = [(i, i ^ step) for i in range(1, count) if i ^ step > 0]
        out.append(lax.ppermute(value, "section", pairs))
    return out


def pick(values, distance):
    result = values[0]
    for step in range(1, len(values)):
        result = jnp.where(distance == step, values[step], result)
    return result


def dot_t(left, right):
    return lax.dot_general(left, right, (((1,), (1,)), ((), ())), preferred_element_type=F32)


def per_device(
    activations,
    top_grad,
    loss_mask,
    norm_gain,
    value_weight,
    output_weight,
    value_proj,
    grad_proj,
    store,
):
    sections = lax.axis_size("section")
    section = lax.axis_index("section")
    shards = lax.axis_size("shard")
    shard = lax.axis_index("shard")
    hidden = activations[0]
    tokens, width = hidden.shape
    kv = value_weight.shape[2]
    proj = value_proj.shape[2]
    columns = width // shards
    half = shards // 2
    groups = sections - 1
    rows = -(-tokens // groups)
    rows = -(-rows // 16) * 16
    padded = rows * groups
    block = shards * rows
    group = jnp.maximum(section - 1, 0)

    gain = norm_gain[0]
    gain_slice = lax.dynamic_slice_in_dim(gain, shard * columns, columns, 0)
    value_scaled = (value_weight[0].astype(F32) * gain_slice[:, None]).astype(BF16)

    hidden_padded = jnp.pad(hidden, ((0, padded - tokens), (0, 0)))

    def rows_of(array, which):
        return lax.dynamic_slice_in_dim(array, which * rows, rows, 0)

    hidden_rows = [rows_of(hidden_padded, group)]
    for step in range(1, sections):
        pairs = [(i, i ^ step) for i in range(1, sections) if i ^ step > 0]
        sent = rows_of(hidden_padded, jnp.maximum((section ^ step) - 1, 0))
        hidden_rows.append(lax.ppermute(sent, "section", pairs))

    output_from = exchange(output_weight[0])
    value_from = exchange(value_scaled)
    proj_slice = lax.dynamic_slice_in_dim(grad_proj[0], shard * columns, columns, 0)
    proj_from = [proj_slice] + [swap(proj_slice, "section", step) for step in range(1, sections)]

    cotangent = (top_grad.astype(F32) * loss_mask.astype(F32)[:, None]).astype(BF16)
    cotangent_rows = rows_of(jnp.pad(cotangent, ((0, padded - tokens), (0, 0))), group)
    state = spread(cotangent_rows).reshape(block, columns).astype(F32)

    layer_rows = jnp.concatenate([pick(hidden_rows, layer ^ section) for layer in range(1, sections)])
    layer_f32 = layer_rows.astype(F32).reshape(groups, rows, width)
    inverse_rows = lax.rsqrt(jnp.mean(layer_f32 * layer_f32, axis=-1, keepdims=True) + EPSILON)
    layer_columns = spread(layer_rows)
    layer_columns = layer_columns.reshape(2, half, groups, rows, columns)

    def hidden_of(layer):
        return layer_columns[:, :, layer - 1].reshape(block, columns)

    hidden_f32 = hidden.astype(F32)
    inverse = lax.rsqrt(jnp.mean(hidden_f32 * hidden_f32, axis=-1, keepdims=True) + EPSILON)
    normed = (hidden_f32 * inverse * gain).astype(BF16)
    low_slice = jnp.dot(value_weight[0], value_proj[0], preferred_element_type=F32).astype(BF16)
    low_full = lax.all_gather(low_slice, "shard", axis=0, tiled=True)
    value_low = jnp.dot(normed, low_full, preferred_element_type=F32)
    grad_low_top = jnp.dot(cotangent, grad_proj[0], preferred_element_type=F32)

    def by_shard(value):
        return value.reshape(2, half, rows, value.shape[1])

    low_parts = []
    scalar = None
    for layer in range(sections - 1, 0, -1):
        output_layer = pick(output_from, layer ^ section)
        value_layer = pick(value_from, layer ^ section)
        inverse_layer = inverse_rows[layer - 1]
        sent = [dot_t(state.astype(BF16), output_layer).astype(BF16)]
        if scalar is not None:
            sent.append(dot_t(hidden_of(layer + 1), output_layer).astype(BF16))
            sent.append(jnp.broadcast_to(scalar, (block, 128)).astype(BF16))
        total = scatter_sum(by_shard(jnp.concatenate(sent, axis=1)))
        grad_value = total[:, :kv]
        if scalar is not None:
            inverse_above = inverse_rows[layer]
            factor = total[:, 2 * kv : 2 * kv + 1] * (inverse_above * inverse_above / width)
            grad_value = grad_value - factor * total[:, kv : 2 * kv]
        back = [(grad_value * inverse_layer).astype(BF16)]
        if scalar is not None:
            back.append(jnp.broadcast_to(factor, (rows, 128)).astype(BF16))
        full = gather_rows(jnp.concatenate(back, axis=1)).reshape(block, -1)
        if scalar is not None:
            state = state - full[:, kv : kv + 1].astype(F32) * hidden_of(layer + 1).astype(F32)
            low_parts.append(
                jnp.dot(state.astype(BF16), pick(proj_from, layer ^ section), preferred_element_type=F32)
            )
        change = dot_t(full[:, :kv], value_layer)
        state = state + change
        scalar = jnp.sum(change * hidden_of(layer).astype(F32), axis=1, keepdims=True)
    proj_first = pick(proj_from, section)
    low_parts.append(jnp.dot(state.astype(BF16), proj_first, preferred_element_type=F32))
    low_parts.append(jnp.dot(hidden_of(1), proj_first, preferred_element_type=F32))
    low_parts.append(jnp.broadcast_to(scalar, (block, proj)))
    low = scatter_sum(by_shard(jnp.concatenate(low_parts, axis=1)))
    low = low.reshape(rows, sections + 1, proj)
    inverse_first = inverse_rows[0]
    factor = low[:, sections, :1] * (inverse_first * inverse_first / width)
    low_first = low[:, sections - 2] - factor * low[:, sections - 1]
    low_layers = jnp.stack([low_first] + [low[:, sections - 2 - layer] for layer in range(1, sections - 1)] + [low_first])

    own = lax.dynamic_index_in_dim(low_layers, section, 0, keepdims=False)
    got = [own]
    for step in range(1, sections):
        got.append(
            swap(lax.dynamic_index_in_dim(low_layers, section ^ step, 0, keepdims=False), "section", step)
        )
    got = jnp.stack(got)
    grad_low = jnp.concatenate(
        [lax.dynamic_index_in_dim(got, section ^ source, 0, keepdims=False) for source in range(1, sections)]
    )[:tokens]
    grad_low = jnp.where(section == sections - 1, grad_low_top, grad_low)

    gens = tokens // LEN
    features = jnp.einsum(
        "gta,gtb->gab",
        grad_low.reshape(gens, LEN, proj),
        value_low.reshape(gens, LEN, proj),
        precision=lax.Precision.HIGHEST,
    ).reshape(gens, proj * proj)
    gathered = gather_rows(features)
    gathered = gathered.transpose(1, 0, 2, 3).reshape(shards, gens, proj * proj)
    gathered = jnp.stack(
        [lax.dynamic_index_in_dim(gathered, shard ^ i, 0, keepdims=False) for i in range(shards)]
    ).reshape(shards * gens, proj * proj)
    partial = lax.dot_general(
        gathered,
        store[0],
        (((1,), (1,)), ((), ())),
        precision=lax.Precision.HIGHEST,
        preferred_element_type=F32,
    )
    rows_out = partial.shape[0] // sections
    result = lax.dynamic_slice_in_dim(partial, section * rows_out, rows_out, 0)
    for step in range(1, sections):
        sent = lax.dynamic_slice_in_dim(partial, (section ^ step) * rows_out, rows_out, 0)
        result = result + swap(sent, "section", step)
    return result


def solution(mesh):
    placed = (
        P("section", "shard", None),
        P("shard", None),
        P("shard"),
        P("section", None),
        P("section", "shard", None),
        P("section", None, "shard"),
        P("section", None, None),
        P("section", None, None),
        P("section", "shard", None),
    )
    return jax.shard_map(
        per_device, mesh=mesh, in_specs=placed, out_specs=P("section", "shard"), check_vma=False
    )
```

time: 327 us -> 266 us (0.81)
  waiting for transfers between devices: 271 us -> 56.2 us
  starting transfers between devices: 4.07 us -> 136 us
  other arithmetic: 3.83 us -> 22.9 us
  local copies, waits for them, and re-layouts: 4.42 us -> 18.2 us
  between operations: 13.5 us -> 1.06 us
  matrix products: 8.57 us -> 14.4 us
  blocking collectives: 21.4 us -> 16.1 us
    all_gather x2 -> x0, waiting for transfers between devices: 159 us -> none  [the longest x1 81.9 us: per_device(): lax.all_gather(value_local, 'shard', axis=0, tiled=True)]
    ppermute x3 -> x58, starting transfers between devices: 4.03 us -> 136 us  [the longest x49 128 us: swap(): lax.ppermute(value, axis, [(i, i ^ step) for i in range(lax.axis_size(axi...]
    ppermute x3 -> x58, waiting for transfers between devices: 111 us -> 56.2 us  [the longest x49 56.1 us: swap(): lax.ppermute(value, axis, [(i, i ^ step) for i in range(lax.axis_size(axi...]
    psum x1 -> x0, blocking collectives: 7.46 us -> none  [per_device(): score_total = lax.psum(partial_value, 'section')]
    another operation x0 -> x24, other arithmetic: none -> 6.33 us  [the longest x6 2.36 us: spread(): got.append(swap(jnp.stack([part[z] for part in both]), 'shard', 2 * z))]
    dot_general x3 -> x16, matrix products: 6.85 us -> 12.7 us  [the longest x8 5.21 us: dot_t(): lax.dot_general(left, right, (((1,), (1,)), ((), ())), preferred_element_...]
    unnamed x10 -> x77, local copies, waits for them, and re-layouts: 0.02 us -> 5.63 us
    add x0 -> x5, other arithmetic: none -> 5.4 us  [the longest x3 3.88 us: scatter_sum(): total = total + swap(pair[z], 'shard', 2 * z).astype(F32)]
  transfers between devices with their start and end apart: 5 -> 58, of which waited for: 5 -> 28; matrix products, arithmetic and copies ran while one was open for 3% -> 10% of each run, Pallas kernels for 0% -> 0%
where the time goes in v1:
time: 266 us; the launch traced here: 265 us
  starting transfers between devices  136 us (51%)
  waiting for transfers between devices  56.2 us (21%)
  other arithmetic  22.9 us (9%)
  local copies, waits for them, and re-layouts  18.2 us (7%)
  blocking collectives  16.1 us (6%)
  matrix products  14.4 us (5%)
    ppermute x49, starting transfers between devices, swap(): lax.ppermute(value, axis, [(i, i ^ step) for i in range(lax.axis_size(axi...  128 us
    ppermute x49, waiting for transfers between devices, swap(): lax.ppermute(value, axis, [(i, i ^ step) for i in range(lax.axis_size(axi...  56.1 us
    all_gather x1, blocking collectives, per_device(): low_full = lax.all_gather(low_slice, 'shard', axis=0, tiled=True)  16.1 us
    unnamed x77, local copies, waits for them, and re-layouts  5.63 us
  transfers between devices with their start and end apart: 58, of which 28 were waited for; matrix products, arithmetic and copies ran while one was open for 10% of the time, Pallas kernels for 0%

profile of v1, /device:TPU:0, one launch (start us, length us, event | category | flops | bytes accessed | tf_op | source)
XLA Modules:
  0.0 265.2 jit_solution(11870749797241325318)
XLA Ops:
  12.0 2.6 collective-permute-start.1
  15.3 2.6 collective-permute-start.2
  18.7 2.4 collective-permute-start.3
  32.4 3.0 %collective-permute-start.23 = (bf16[2,96,512]{2,1,0:T(8,128)(2,1)S(1)}, bf16[2,96,512]{2,1,0:T(8,128)(2,1)S(1)}, u32[]{:S(2)}, u32[]{:S(2)}) collective-permute-start(bf16[2,96,512]{2,1,0:T(8,128)(2,1)S(1)} %pad_maximum_fusion.13), channel_id=1, source_target_pairs={{0,4},{1,5},{2,6},{3,7},{4,0},{5,1},{6,2},{7,3},{8,12},{9,13},{10,... | collective-permute-start | bytes 589832 | tf_op jit(solution)/shard_map/ppermute | solution.py:13
  37.0 6.3 %collective-permute-done.22 = bf16[2,96,512]{2,1,0:T(8,128)(2,1)S(1)} collective-permute-done((bf16[2,96,512]{2,1,0:T(8,128)(2,1)S(1)}, bf16[2,96,512]{2,1,0:T(8,128)(2,1)S(1)}, u32[]{:S(2)}, u32[]{:S(2)}) %collective-permute-start.22) | collective-permute-done | bytes 196640 | tf_op jit(solution)/shard_map/ppermute | solution.py:13
  44.8 6.1 %collective-permute-done.23 = bf16[2,96,512]{2,1,0:T(8,128)(2,1)S(1)} collective-permute-done((bf16[2,96,512]{2,1,0:T(8,128)(2,1)S(1)}, bf16[2,96,512]{2,1,0:T(8,128)(2,1)S(1)}, u32[]{:S(2)}, u32[]{:S(2)}) %collective-permute-start.23) | collective-permute-done | bytes 196640 | tf_op jit(solution)/shard_map/ppermute | solution.py:13
  50.9 5.8 %collective-permute-start.9 = (bf16[32,1024]{1,0:T(8,128)(2,1)S(1)}, bf16[32,1024]{1,0:T(8,128)(2,1)S(1)}, u32[]{:S(2)}, u32[]{:S(2)}) collective-permute-start(bf16[32,1024]{1,0:T(8,128)(2,1)S(1)} %get-tuple-element.62), channel_id=1, source_target_pairs={{0,4},{1,5},{2,6},{3,7},{4,0},{5,1},{6,2},{7,3},{8,12},{9,13},{10,... | collective-permute-start | bytes 196616 | tf_op jit(solution)/shard_map/ppermute | solution.py:13
  63.5 2.3 collective-permute-start.16
  67.6 2.0 collective-permute-done.16
  78.6 2.1 collective-permute-start.27
  82.4 4.0 %collective-permute-done.26 = bf16[32,2176]{1,0:T(8,128)(2,1)S(1)} collective-permute-done((bf16[32,2176]{1,0:T(8,128)(2,1)}, bf16[32,2176]{1,0:T(8,128)(2,1)S(1)}, u32[]{:S(2)}, u32[]{:S(2)}) %collective-permute-start.26) | collective-permute-done | bytes 139296 | tf_op jit(solution)/shard_map/ppermute | solution.py:13
  86.3 6.0 %collective-permute-done.27 = bf16[32,2176]{1,0:T(8,128)(2,1)} collective-permute-done((bf16[32,2176]{1,0:T(8,128)(2,1)}, bf16[32,2176]{1,0:T(8,128)(2,1)}, u32[]{:S(2)}, u32[]{:S(2)}) %collective-permute-start.27) | collective-permute-done | bytes 139296 | tf_op jit(solution)/shard_map/ppermute | solution.py:13
  93.8 2.5 collective-permute-start.29
  99.1 5.3 %collective-permute-done.30 = bf16[32,1152]{1,0:T(8,128)(2,1)S(1)} collective-permute-done((bf16[32,1152]{1,0:T(8,128)(2,1)S(1)}, bf16[32,1152]{1,0:T(8,128)(2,1)S(1)}, u32[]{:S(2)}, u32[]{:S(2)}) %collective-permute-start.30) | collective-permute-done | bytes 73760 | tf_op jit(solution)/shard_map/ppermute | solution.py:13
  118.9 59.1 %collective-permute-start.33 = (bf16[512,64]{0,1:T(8,128)(2,1)}, bf16[512,64]{0,1:T(8,128)(2,1)S(1)}, u32[]{:S(2)}, u32[]{:S(2)}) collective-permute-start(bf16[512,64]{0,1:T(8,128)(2,1)} %dynamic-slice_bitcast_fusion.10), channel_id=1, source_target_pairs={{0,24},{8,16},{16,8},{24,0},{1,25},{9,17},{17,9},{25,1},{2,26},{10... | collective-permute-start | bytes 196616 | tf_op jit(solution)/shard_map/ppermute | solution.py:13
  181.9 2.3 collective-permute-start.41
  199.0 16.1 %all_gather.3 = bf16[4096,64]{0,1:T(8,128)(2,1)} all-gather(bf16[512,64]{0,1:T(8,128)(2,1)S(1)} %copy-done.22), channel_id=1, replica_groups=mesh['section'=4,'shard'=8] {'shard'}, dimensions={0}, use_global_device_ids=true | all-gather | bytes 589824 | tf_op jit(solution)/shard_map/all_gather | solution.py:134
  218.1 2.4 collective-permute-start.46
  231.5 9.9 %collective-permute-start.49 = (f32[32,64]{1,0:T(8,128)S(1)}, f32[32,64]{1,0:T(8,128)S(1)}, u32[]{:S(2)}, u32[]{:S(2)}) collective-permute-start(f32[32,64]{1,0:T(8,128)S(1)} %get-tuple-element.83), channel_id=1, source_target_pairs={{0,16},{8,24},{16,0},{24,8},{1,17},{9,25},{17,1},{25,9},{2,18},{10... | collective-permute-start | bytes 24584 | tf_op jit(solution)/shard_map/ppermute | solution.py:13
  243.1 2.9 %collective-permute-done.50 = f32[32,64]{1,0:T(8,128)S(1)} collective-permute-done((f32[32,64]{1,0:T(8,128)S(1)}, f32[32,64]{1,0:T(8,128)S(1)}, u32[]{:S(2)}, u32[]{:S(2)}) %collective-permute-start.50) | collective-permute-done | bytes 8224 | tf_op jit(solution)/shard_map/ppermute | solution.py:13
  248.2 2.4 collective-permute-start.52
  250.6 2.0 collective-permute-start.53
  252.9 3.2 %collective-permute-done.53 = f32[1,4096]{1,0:T(1,128)S(1)} collective-permute-done((f32[1,4096]{1,0:T(1,128)S(1)}, f32[1,4096]{1,0:T(1,128)S(1)}, u32[]{:S(2)}, u32[]{:S(2)}) %collective-permute-start.53) | collective-permute-done | bytes 16416 | tf_op jit(solution)/shard_map/ppermute | solution.py:13
  260.2 2.9 %collective-permute-start.57 = (f32[2,128]{1,0:T(2,128)S(1)}, f32[2,128]{1,0:T(2,128)S(1)}, u32[]{:S(2)}, u32[]{:S(2)}) collective-permute-start(f32[2,128]{1,0:T(2,128)S(1)} %get-tuple-element.86), channel_id=1, source_target_pairs={{0,24},{8,16},{16,8},{24,0},{1,25},{9,17},{17,9},{25,1},{2,26},{10... | collective-permute-start | bytes 3080 | tf_op jit(solution)/shard_map/ppermute | solution.py:13
  (283 shorter events, 108.1 us)
Async XLA Ops:
  5.9 19.7 %collective-permute-start.11 = (bf16[32,4096]{1,0:T(8,128)(2,1)}, bf16[32,4096]{1,0:T(8,128)(2,1)S(1)}, u32[]{:S(2)}, u32[]{:S(2)}) collective-permute-start(bf16[32,4096]{1,0:T(8,128)(2,1)} %get-tuple-element.37), channel_id=1, source_target_pairs={{8,16},{16,8},{9,17},{17,9},{10,18},{18,10},{11,19},{19,11},{12,20... | collective-permute-start | bytes 786440 | tf_op jit(solution)/shard_map/ppermute | solution.py:110
  6.6 19.8 %collective-permute-start.12 = (bf16[32,4096]{1,0:T(8,128)(2,1)}, bf16[32,4096]{1,0:T(8,128)(2,1)}, u32[]{:S(2)}, u32[]{:S(2)}) collective-permute-start(bf16[32,4096]{1,0:T(8,128)(2,1)} %get-tuple-element.36), channel_id=1, source_target_pairs={{8,24},{24,8},{9,25},{25,9},{10,26},{26,10},{11,27},{27,11},{12,28... | collective-permute-start | bytes 786440 | tf_op jit(solution)/shard_map/ppermute | solution.py:110
  7.9 19.1 %collective-permute-start.13 = (bf16[32,4096]{1,0:T(8,128)(2,1)S(1)}, bf16[32,4096]{1,0:T(8,128)(2,1)}, u32[]{:S(2)}, u32[]{:S(2)}) collective-permute-start(bf16[32,4096]{1,0:T(8,128)(2,1)S(1)} %get-tuple-element.35), channel_id=1, source_target_pairs={{16,24},{24,16},{17,25},{25,17},{18,26},{26,18},{19,27},{27,19},{2... | collective-permute-start | bytes 786440 | tf_op jit(solution)/shard_map/ppermute | solution.py:110
  22.2 9.2 %collective-permute-start.4 = (bf16[1024,512]{1,0:T(8,128)(2,1)}, bf16[1024,512]{1,0:T(8,128)(2,1)S(1)}, u32[]{:S(2)}, u32[]{:S(2)}) collective-permute-start(bf16[1024,512]{1,0:T(8,128)(2,1)} %bitcast.265), channel_id=1, source_target_pairs={{8,16},{16,8},{9,17},{17,9},{10,18},{18,10},{11,19},{19,11},{12,20... | collective-permute-start | bytes 3145736 | tf_op jit(solution)/shard_map/ppermute | solution.py:54
  26.3 45.0 %collective-permute-start.18 = (bf16[512,1024]{1,0:T(8,128)(2,1)}, bf16[512,1024]{1,0:T(8,128)(2,1)S(1)}, u32[]{:S(2)}, u32[]{:S(2)}) collective-permute-start(bf16[512,1024]{1,0:T(8,128)(2,1)} %multiply_convert_fusion), channel_id=1, source_target_pairs={{8,16},{16,8},{9,17},{17,9},{10,18},{18,10},{11,19},{19,11},{12,20... | collective-permute-start | bytes 3145736 | tf_op jit(solution)/shard_map/ppermute | solution.py:54
  30.6 40.8 %collective-permute-start.19 = (bf16[512,1024]{1,0:T(8,128)(2,1)S(1)}, bf16[512,1024]{1,0:T(8,128)(2,1)S(1)}, u32[]{:S(2)}, u32[]{:S(2)}) collective-permute-start(bf16[512,1024]{1,0:T(8,128)(2,1)S(1)} %copy-done.17), channel_id=1, source_target_pairs={{8,24},{24,8},{9,25},{25,9},{10,26},{26,10},{11,27},{27,11},{12,28... | collective-permute-start | bytes 3145736 | tf_op jit(solution)/shard_map/ppermute | solution.py:54
  32.3 11.0 %collective-permute-start.22 = (bf16[2,96,512]{2,1,0:T(8,128)(2,1)S(1)}, bf16[2,96,512]{2,1,0:T(8,128)(2,1)S(1)}, u32[]{:S(2)}, u32[]{:S(2)}) collective-permute-start(bf16[2,96,512]{2,1,0:T(8,128)(2,1)S(1)} %pad_maximum_fusion.12), channel_id=1, source_target_pairs={{0,2},{1,3},{2,0},{3,1},{4,6},{5,7},{6,4},{7,5},{8,10},{9,11},{10,... | collective-permute-start | bytes 589832 | tf_op jit(solution)/shard_map/ppermute | solution.py:13
  32.4 18.6 %collective-permute-start.23 = (bf16[2,96,512]{2,1,0:T(8,128)(2,1)S(1)}, bf16[2,96,512]{2,1,0:T(8,128)(2,1)S(1)}, u32[]{:S(2)}, u32[]{:S(2)}) collective-permute-start(bf16[2,96,512]{2,1,0:T(8,128)(2,1)S(1)} %pad_maximum_fusion.13), channel_id=1, source_target_pairs={{0,4},{1,5},{2,6},{3,7},{4,0},{5,1},{6,2},{7,3},{8,12},{9,13},{10,... | collective-permute-start | bytes 589832 | tf_op jit(solution)/shard_map/ppermute | solution.py:13
  35.4 15.6 %collective-permute-start.24 = (bf16[2,96,512]{2,1,0:T(8,128)(2,1)S(1)}, bf16[2,96,512]{2,1,0:T(8,128)(2,1)S(1)}, u32[]{:S(2)}, u32[]{:S(2)}) collective-permute-start(bf16[2,96,512]{2,1,0:T(8,128)(2,1)S(1)} %pad_maximum_fusion.14), channel_id=1, source_target_pairs={{0,6},{1,7},{2,4},{3,5},{4,2},{5,3},{6,0},{7,1},{8,14},{9,15},{10,... | collective-permute-start | bytes 589832 | tf_op jit(solution)/shard_map/ppermute | solution.py:13
  43.3 13.5 %collective-permute-start.10 = (bf16[32,1024]{1,0:T(8,128)(2,1)S(1)}, bf16[32,1024]{1,0:T(8,128)(2,1)S(1)}, u32[]{:S(2)}, u32[]{:S(2)}) collective-permute-start(bf16[32,1024]{1,0:T(8,128)(2,1)S(1)} %get-tuple-element.61), channel_id=1, source_target_pairs={{0,6},{1,7},{2,4},{3,5},{4,2},{5,3},{6,0},{7,1},{8,14},{9,15},{10,... | collective-permute-start | bytes 196616 | tf_op jit(solution)/shard_map/ppermute | solution.py:13
  50.9 8.1 %collective-permute-start.9 = (bf16[32,1024]{1,0:T(8,128)(2,1)S(1)}, bf16[32,1024]{1,0:T(8,128)(2,1)S(1)}, u32[]{:S(2)}, u32[]{:S(2)}) collective-permute-start(bf16[32,1024]{1,0:T(8,128)(2,1)S(1)} %get-tuple-element.62), channel_id=1, source_target_pairs={{0,4},{1,5},{2,6},{3,7},{4,0},{5,1},{6,2},{7,3},{8,12},{9,13},{10,... | collective-permute-start | bytes 196616 | tf_op jit(solution)/shard_map/ppermute | solution.py:13
  56.8 14.6 %collective-permute-start.20 = (bf16[512,1024]{1,0:T(8,128)(2,1)S(1)}, bf16[512,1024]{1,0:T(8,128)(2,1)S(1)}, u32[]{:S(2)}, u32[]{:S(2)}) collective-permute-start(bf16[512,1024]{1,0:T(8,128)(2,1)S(1)} %copy-done.17), channel_id=1, source_target_pairs={{16,24},{24,16},{17,25},{25,17},{18,26},{26,18},{19,27},{27,19},{2... | collective-permute-start | bytes 3145736 | tf_op jit(solution)/shard_map/ppermute | solution.py:54
  77.9 8.5 %collective-permute-start.26 = (bf16[32,2176]{1,0:T(8,128)(2,1)}, bf16[32,2176]{1,0:T(8,128)(2,1)S(1)}, u32[]{:S(2)}, u32[]{:S(2)}) collective-permute-start(bf16[32,2176]{1,0:T(8,128)(2,1)} %get-tuple-element.41), channel_id=1, source_target_pairs={{0,2},{1,3},{2,0},{3,1},{4,6},{5,7},{6,4},{7,5},{8,10},{9,11},{10,... | collective-permute-start | bytes 417800 | tf_op jit(solution)/shard_map/ppermute | solution.py:13
  78.6 13.7 %collective-permute-start.27 = (bf16[32,2176]{1,0:T(8,128)(2,1)}, bf16[32,2176]{1,0:T(8,128)(2,1)}, u32[]{:S(2)}, u32[]{:S(2)}) collective-permute-start(bf16[32,2176]{1,0:T(8,128)(2,1)} %get-tuple-element.43), channel_id=1, source_target_pairs={{0,4},{1,5},{2,6},{3,7},{4,0},{5,1},{6,2},{7,3},{8,12},{9,13},{10,... | collective-permute-start | bytes 417800 | tf_op jit(solution)/shard_map/ppermute | solution.py:13
  80.7 11.6 %collective-permute-start.28 = (bf16[32,2176]{1,0:T(8,128)(2,1)S(1)}, bf16[32,2176]{1,0:T(8,128)(2,1)}, u32[]{:S(2)}, u32[]{:S(2)}) collective-permute-start(bf16[32,2176]{1,0:T(8,128)(2,1)S(1)} %get-tuple-element.42), channel_id=1, source_target_pairs={{0,6},{1,7},{2,4},{3,5},{4,2},{5,3},{6,0},{7,1},{8,14},{9,15},{10,... | collective-permute-start | bytes 417800 | tf_op jit(solution)/shard_map/ppermute | solution.py:13
  96.4 8.0 %collective-permute-start.30 = (bf16[32,1152]{1,0:T(8,128)(2,1)S(1)}, bf16[32,1152]{1,0:T(8,128)(2,1)S(1)}, u32[]{:S(2)}, u32[]{:S(2)}) collective-permute-start(bf16[32,1152]{1,0:T(8,128)(2,1)S(1)} %get-tuple-element.77), channel_id=1, source_target_pairs={{0,4},{1,5},{2,6},{3,7},{4,0},{5,1},{6,2},{7,3},{8,12},{9,13},{10,... | collective-permute-start | bytes 221192 | tf_op jit(solution)/shard_map/ppermute | solution.py:13
  113.0 65.6 %collective-permute-start.37 = (bf16[32,2176]{1,0:T(8,128)(2,1)}, bf16[32,2176]{1,0:T(8,128)(2,1)}, u32[]{:S(2)}, u32[]{:S(2)}) collective-permute-start(bf16[32,2176]{1,0:T(8,128)(2,1)} %get-tuple-element.38), channel_id=1, source_target_pairs={{0,2},{1,3},{2,0},{3,1},{4,6},{5,7},{6,4},{7,5},{8,10},{9,11},{10,... | collective-permute-start | bytes 417800 | tf_op jit(solution)/shard_map/ppermute | solution.py:13
  114.4 64.3 %collective-permute-start.38 = (bf16[32,2176]{1,0:T(8,128)(2,1)}, bf16[32,2176]{1,0:T(8,128)(2,1)}, u32[]{:S(2)}, u32[]{:S(2)}) collective-permute-start(bf16[32,2176]{1,0:T(8,128)(2,1)} %get-tuple-element.40), channel_id=1, source_target_pairs={{0,4},{1,5},{2,6},{3,7},{4,0},{5,1},{6,2},{7,3},{8,12},{9,13},{10,... | collective-permute-start | bytes 417800 | tf_op jit(solution)/shard_map/ppermute | solution.py:13
  116.0 62.6 %collective-permute-start.39 = (bf16[32,2176]{1,0:T(8,128)(2,1)}, bf16[32,2176]{1,0:T(8,128)(2,1)}, u32[]{:S(2)}, u32[]{:S(2)}) collective-permute-start(bf16[32,2176]{1,0:T(8,128)(2,1)} %get-tuple-element.39), channel_id=1, source_target_pairs={{0,6},{1,7},{2,4},{3,5},{4,2},{5,3},{6,0},{7,1},{8,14},{9,15},{10,... | collective-permute-start | bytes 417800 | tf_op jit(solution)/shard_map/ppermute | solution.py:13
  118.9 73.1 %collective-permute-start.33 = (bf16[512,64]{0,1:T(8,128)(2,1)}, bf16[512,64]{0,1:T(8,128)(2,1)S(1)}, u32[]{:S(2)}, u32[]{:S(2)}) collective-permute-start(bf16[512,64]{0,1:T(8,128)(2,1)} %dynamic-slice_bitcast_fusion.10), channel_id=1, source_target_pairs={{0,24},{8,16},{16,8},{24,0},{1,25},{9,17},{17,9},{25,1},{2,26},{10... | collective-permute-start | bytes 196616 | tf_op jit(solution)/shard_map/ppermute | solution.py:13
  177.9 14.0 %collective-permute-start.34 = (bf16[512,64]{0,1:T(8,128)(2,1)}, bf16[512,64]{0,1:T(8,128)(2,1)S(1)}, u32[]{:S(2)}, u32[]{:S(2)}) collective-permute-start(bf16[512,64]{0,1:T(8,128)(2,1)} %dynamic-slice_bitcast_fusion.10), channel_id=1, source_target_pairs={{0,16},{8,24},{16,0},{24,8},{1,17},{9,25},{17,1},{25,9},{2,18},{10... | collective-permute-start | bytes 196616 | tf_op jit(solution)/shard_map/ppermute | solution.py:13
  198.8 17.2 %collective-permute-start.44 = (f32[4,32,320]{2,1,0:T(8,128)}, f32[4,32,320]{2,1,0:T(8,128)}, u32[]{:S(2)}, u32[]{:S(2)}) collective-permute-start(f32[4,32,320]{2,1,0:T(8,128)} %bitcast.296), channel_id=1, source_target_pairs={{0,1},{1,0},{2,3},{3,2},{4,5},{5,4},{6,7},{7,6},{8,9},{9,8},{10,11... | collective-permute-start | bytes 491528 | tf_op jit(solution)/shard_map/ppermute | solution.py:13
  230.0 12.9 %collective-permute-start.48 = (f32[32,64]{1,0:T(8,128)S(1)}, f32[32,64]{1,0:T(8,128)S(1)}, u32[]{:S(2)}, u32[]{:S(2)}) collective-permute-start(f32[32,64]{1,0:T(8,128)S(1)} %get-tuple-element.84), channel_id=1, source_target_pairs={{0,8},{8,0},{16,24},{24,16},{1,9},{9,1},{17,25},{25,17},{2,10},{10... | collective-permute-start | bytes 24584 | tf_op jit(solution)/shard_map/ppermute | solution.py:13
  231.5 11.6 %collective-permute-start.49 = (f32[32,64]{1,0:T(8,128)S(1)}, f32[32,64]{1,0:T(8,128)S(1)}, u32[]{:S(2)}, u32[]{:S(2)}) collective-permute-start(f32[32,64]{1,0:T(8,128)S(1)} %get-tuple-element.83), channel_id=1, source_target_pairs={{0,16},{8,24},{16,0},{24,8},{1,17},{9,25},{17,1},{25,9},{2,18},{10... | collective-permute-start | bytes 24584 | tf_op jit(solution)/shard_map/ppermute | solution.py:13
  (69 other events, 679.8 us)

commit v2 on v0

v2 whole, which is shorter than its diff:
```python
import jax
import jax.numpy as jnp
from jax import lax
from jax.experimental import pallas as pl
from jax.experimental.pallas import tpu as pltpu
from jax.sharding import PartitionSpec as P

LEN = 96
EPSILON = 1e-05
BF16 = jnp.bfloat16
F32 = jnp.float32


def swap(value, axis, step):
    return lax.ppermute(value, axis, [(i, i ^ step) for i in range(lax.axis_size(axis))])


def radices(count):
    digits = []
    while count > 1:
        digit = 4 if count % 4 == 0 else 2
        digits.append(digit)
        count //= digit
    return digits


def step_list(rest, digit):
    return [2 * rest * place for place in range(1, digit)]


def scatter_terms(parts):
    digits = radices(parts.shape[0])
    for place, digit in enumerate(digits):
        rest = parts.shape[0] // digit
        split = parts.reshape((digit, rest) + parts.shape[1:])
        got = [split[0]] + [swap(split[j + 1], "shard", step) for j, step in enumerate(step_list(rest, digit))]
        if place == len(digits) - 1:
            return [value.reshape(parts.shape[1:]) for value in got]
        parts = sum(value.astype(F32) for value in got).astype(parts.dtype)
    return [parts.reshape(parts.shape[1:])]


def scatter_sum(parts):
    return sum(value.astype(F32) for value in scatter_terms(parts))


def gather_pieces(rows):
    values = [rows]
    chips = lax.axis_size("shard") // 2
    for digit in reversed(radices(chips)):
        value = values[0] if len(values) == 1 else jnp.concatenate(values)
        rest = value.shape[0] // rows.shape[0]
        values = [value] + [swap(value, "shard", step) for step in step_list(rest, digit)]
    return values


def gather_chips(rows):
    return jnp.concatenate(gather_pieces(rows)).reshape((-1,) + rows.shape)


def spread(pieces):
    chips = pieces.shape[0]
    tail = pieces.shape[1:]
    done = 1
    value = pieces.reshape((1, chips) + tail)
    for digit in radices(chips):
        rest = value.shape[1] // digit
        value = value.reshape((done, digit, rest) + tail)
        got = [value[:, 0]]
        for j, step in enumerate(step_list(rest, digit)):
            got.append(swap(value[:, j + 1], "shard", step))
        value = jnp.stack(got, axis=1)
        done = done * digit
        value = value.reshape((done, rest) + tail)
    return value.reshape((chips,) + tail)


def exchange(value, steps, sections):
    return {
        step: lax.ppermute(value, "section", [(i, i ^ step) for i in range(1, sections) if i ^ step > 0])
        for step in steps
    }


def ways(layer, sections):
    return sorted(layer ^ other for other in range(1, sections))


def choose_body(which, *refs):
    *sources, target, sem = refs
    for place, source in enumerate(sources):

        @pl.when(which[0] == place)
        def _():
            copy = pltpu.make_async_copy(source, target, sem)
            copy.start()
            copy.wait()


def choose(values, layer, section, sections):
    keys = ways(layer, sections)
    which = jnp.int32(0)
    for place, key in enumerate(keys):
        which = jnp.where((layer ^ section) == key, place, which)
    value = values[keys[0]]
    return pl.pallas_call(
        choose_body,
        out_shape=jax.ShapeDtypeStruct(value.shape, value.dtype),
        in_specs=[pl.BlockSpec(memory_space=pltpu.SMEM)] + [pl.BlockSpec(memory_space=pl.ANY)] * len(keys),
        out_specs=pl.BlockSpec(memory_space=pltpu.VMEM),
        scratch_shapes=[pltpu.SemaphoreType.DMA],
        cost_estimate=pl.CostEstimate(flops=0, bytes_accessed=2 * value.size * 2, transcendentals=0),
    )(which.reshape(1), *[values[key] for key in keys])


def pick(values, layer, section, sections):
    keys = ways(layer, sections)
    distance = layer ^ section
    result = values[keys[0]]
    for key in keys[1:]:
        result = jnp.where(distance == key, values[key], result)
    return result


def dot_t(left, right):
    return lax.dot_general(left, right, (((1,), (1,)), ((), ())), preferred_element_type=F32)


PARAMS = pltpu.CompilerParams(vmem_limit_bytes=36 * 1024 * 1024)


def rows_body(width, *refs):
    *addends, act, out = refs
    kv = addends[0].shape[1]
    total = addends[0][...].astype(F32)
    for value in addends[1:]:
        total = total + value[...].astype(F32)
    inverse = act[:, kv : kv + 1].astype(F32) + act[:, kv + 64 : kv + 65].astype(F32)
    grad_value = total * inverse
    factor = jnp.sum(grad_value * act[:, :kv].astype(F32), axis=1, keepdims=True) * inverse / width
    out[:, :kv] = grad_value.astype(BF16)
    out[:, kv:] = jnp.broadcast_to(factor, (factor.shape[0], out.shape[1] - kv)).astype(BF16)


def rows_step(addends, act, width):
    rows, kv = addends[0].shape
    return pl.pallas_call(
        lambda *refs: rows_body(width, *refs),
        out_shape=jax.ShapeDtypeStruct(act.shape, BF16),
        compiler_params=PARAMS,
        cost_estimate=pl.CostEstimate(flops=8 * rows * kv, bytes_accessed=16 * rows * kv, transcendentals=0),
    )(*addends, act)


def layer_body(last, *refs):
    *pieces, state, hidden, value_near, value_far, next_near, next_far, new_state, part, full = refs
    kv = value_near.shape[1]
    columns = value_near.shape[0]
    start = 0
    for piece in pieces:
        full[start : start + piece.shape[0]] = piece[...]
        start += piece.shape[0]
    grad = full[:, :kv]
    factor = full[:, kv : kv + 1].astype(F32)
    total = None
    for place, (value, after_value) in enumerate(((value_near, next_near), (value_far, next_far))):
        here = slice(place * columns, (place + 1) * columns)
        change = dot_t(grad, value[...])
        moved = state[:, here] + change - hidden[:, here].astype(F32) * factor
        new_state[:, here] = moved
        term = dot_t(moved.astype(BF16), after_value[...])
        total = term if total is None else total + term
    part[...] = total.astype(part.dtype)


def layer_step(pieces, state, hidden, value_near, value_far, next_near, next_far, part_dtype):
    block, width = state.shape
    kv = value_near.shape[1]
    outs = next_near.shape[0]
    return pl.pallas_call(
        lambda *refs: layer_body(False, *refs),
        out_shape=(
            jax.ShapeDtypeStruct((block, width), F32),
            jax.ShapeDtypeStruct((block, outs), part_dtype),
        ),
        scratch_shapes=[pltpu.VMEM((block, pieces[0].shape[1]), BF16)],
        compiler_params=PARAMS,
        cost_estimate=pl.CostEstimate(
            flops=2 * block * width * (kv + outs),
            bytes_accessed=2 * width * (kv + outs) + 12 * block * width,
            transcendentals=0,
        ),
    )(*pieces, state, hidden, value_near, value_far, next_near, next_far)


def per_device(
    activations,
    top_grad,
    loss_mask,
    norm_gain,
    value_weight,
    output_weight,
    value_proj,
    grad_proj,
    store,
):
    sections = lax.axis_size("section")
    section = lax.axis_index("section")
    shards = lax.axis_size("shard")
    shard = lax.axis_index("shard")
    hidden = activations[0]
    tokens, width = hidden.shape
    kv = value_weight.shape[2]
    proj = value_proj.shape[2]
    columns = width // shards
    chips = shards // 2
    groups = sections - 1
    rows = -(-tokens // groups)
    rows = -(-rows // 16) * 16
    padded = rows * groups
    block = chips * rows
    group = jnp.maximum(section - 1, 0)
    gens = tokens // LEN

    def chip_columns(array, chip):
        first = shard ^ (2 * chip)
        return jnp.concatenate(
            [
                lax.dynamic_slice_in_dim(array, first * columns, columns, 1),
                lax.dynamic_slice_in_dim(array, (first ^ 1) * columns, columns, 1),
            ],
            axis=1,
        )

    near = [step for step in ways(sections - 1, sections) if step]
    far = [step for step in range(1, sections) if step not in near]
    output_from = {0: output_weight[0], **exchange(output_weight[0], near, sections)}

    cotangent = (top_grad.astype(F32) * loss_mask.astype(F32)[:, None]).astype(BF16)
    cotangent_rows = lax.dynamic_slice_in_dim(
        jnp.pad(cotangent, ((0, padded - tokens), (0, 0))), group * rows, rows, 0
    )
    state = spread(jnp.stack([chip_columns(cotangent_rows, chip) for chip in range(chips)]))
    state = state.reshape(block, 2 * columns)

    hidden_columns = spread(jnp.stack([chip_columns(hidden, chip) for chip in range(chips)]))
    gain_slice = lax.dynamic_slice_in_dim(norm_gain[0], shard * columns, columns, 0)
    value_scaled = (value_weight[0].astype(F32) * gain_slice[:, None]).astype(BF16)
    scaled_far = swap(value_scaled, "shard", 1)

    columns_padded = jnp.pad(hidden_columns, ((0, 0), (0, padded - tokens), (0, 0)))

    def to_groups(array, dim):
        def part(other):
            return lax.dynamic_slice_in_dim(array, jnp.maximum(other - 1, 0) * rows, rows, dim)

        out = {0: part(section)}
        for step in range(1, sections):
            pairs = [(i, i ^ step) for i in range(1, sections) if i ^ step > 0]
            out[step] = lax.ppermute(part(section ^ step), "section", pairs)
        return out

    proj_piece = chip_columns(grad_proj[0].T, 0)

    def message(other):
        part = lax.dynamic_slice_in_dim(columns_padded, jnp.maximum(other - 1, 0) * rows, rows, 1)
        return jnp.concatenate([part.reshape(block, 2 * columns), proj_piece])

    message_from = [message(section)]
    for step in range(1, sections):
        pairs = [(i, i ^ step) for i in range(sections) if i ^ step > 0]
        message_from.append(lax.ppermute(message(section ^ step), "section", pairs))

    flat = hidden_columns.reshape(chips * tokens, 2 * columns)
    part = jnp.dot(flat[:, :columns], value_scaled, preferred_element_type=F32)
    part = part + jnp.dot(flat[:, columns:], scaled_far, preferred_element_type=F32)
    value_sum_terms = scatter_terms(part.astype(BF16).reshape(chips, tokens, kv))
    output_from, state = lax.optimization_barrier((output_from, state))
    value_from = {0: value_scaled, **exchange(value_scaled, near, sections)}
    value_sum_terms, value_from = lax.optimization_barrier((value_sum_terms, value_from))
    value_sum = sum(term.astype(F32) for term in value_sum_terms)
    hidden_f32 = hidden.astype(F32)
    inverse = lax.rsqrt(jnp.mean(hidden_f32 * hidden_f32, axis=-1, keepdims=True) + EPSILON)
    value_act = (value_sum * inverse).astype(BF16)
    value_low = jnp.dot(value_act, value_proj[0], preferred_element_type=F32)
    grad_low_top = jnp.dot(cotangent, grad_proj[0], preferred_element_type=F32)
    inverse_high = inverse.astype(BF16)
    inverse_low = (inverse - inverse_high.astype(F32)).astype(BF16)
    value_rows = jnp.concatenate(
        [
            value_act,
            jnp.broadcast_to(inverse_high, (tokens, 64)),
            jnp.broadcast_to(inverse_low, (tokens, 64)),
        ],
        axis=1,
    )

    value_rows, own_output = lax.optimization_barrier((value_rows, output_weight[0]))
    value_rows_from = to_groups(jnp.pad(value_rows, ((0, padded - tokens), (0, 0))), 0)
    far_output = exchange(own_output, far, sections)

    def message_of(layer):
        distance = layer ^ section
        result = message_from[0]
        for step in range(1, sections):
            result = jnp.where(distance == step, message_from[step], result)
        return result

    output_near = choose(output_from, sections - 1, section, sections)
    output_far = swap(output_near, "shard", 1)
    part = dot_t(state[:, :columns], output_near) + dot_t(state[:, columns:], output_far)
    part = part.astype(BF16)
    state = state.astype(F32)
    low_parts = []
    for layer in range(sections - 1, 0, -1):
        terms = scatter_terms(part.reshape(chips, rows, kv))
        if layer == max(sections - 2, 1) and sections > 2:
            terms, mine = lax.optimization_barrier((terms, mine))
        if layer == sections - 1:
            terms, value_rows_from, message_from, own_value = lax.optimization_barrier(
                (terms, value_rows_from, message_from, value_scaled)
            )
            output_from.update(far_output)
            value_from.update(exchange(own_value, far, sections))
            messages = [message_of(place) for place in range(sections)]
        act = pick(value_rows_from, layer, section, sections)
        pieces = gather_pieces(rows_step(terms, act, width))
        value_near = choose(value_from, layer, section, sections)
        value_far = swap(value_near, "shard", 1)
        if layer < sections - 1:
            low_parts.append(dot_t(state.astype(BF16), messages[layer][block:]))
        if layer > 1:
            next_near = choose(output_from, layer - 1, section, sections)
            next_far = swap(next_near, "shard", 1)
        else:
            next_near = messages[0][block:, :columns]
            next_far = messages[0][block:, columns:]
        state, part = layer_step(
            pieces,
            state,
            messages[layer][:block],
            value_near,
            value_far,
            next_near,
            next_far,
            BF16 if layer > 1 else F32,
        )
        if layer == sections - 1:
            mine = gather_chips(jnp.concatenate([value_low, grad_low_top], axis=1))
            mine = jnp.concatenate([mine, swap(mine, "shard", 1)])
    low_parts.append(part)
    low = jnp.concatenate(low_parts, axis=1).astype(BF16)
    low = sum_chips(low.reshape(chips, rows, groups * proj))
    low = jnp.concatenate([low, swap(low, "shard", 1)]).reshape(shards, rows, groups * proj)
    low_layers = jnp.stack(
        [low[:, :, place * proj : (place + 1) * proj] for place in range(groups - 1, -1, -1)] + [low[:, :, :proj]]
    )

    got = [lax.dynamic_index_in_dim(low_layers, section, 0, keepdims=False)]
    for step in range(1, sections):
        got.append(
            swap(
                lax.dynamic_index_in_dim(low_layers, section ^ step, 0, keepdims=False).astype(BF16),
                "section",
                step,
            ).astype(F32)
        )

    def source_rows(source):
        result = got[0]
        for step in range(1, sections):
            result = jnp.where((section ^ source) == step, got[step], result)
        return result

    grad_low = jnp.concatenate([source_rows(source) for source in range(1, sections)], axis=1)[:, :tokens]
    grad_low = jnp.where(section == sections - 1, mine[:, :, proj:], grad_low)

    features = jnp.einsum(
        "gta,gtb->gab",
        grad_low.reshape(shards * gens, LEN, proj),
        mine[:, :, :proj].reshape(shards * gens, LEN, proj),
        precision=lax.Precision.HIGHEST,
    ).reshape(shards * gens, proj * proj)
    partial = lax.dot_general(
        features,
        store[0],
        (((1,), (1,)), ((), ())),
        precision=lax.Precision.HIGHEST,
        preferred_element_type=F32,
    ).reshape(2, chips, gens, -1)

    def of_shard(index):
        away = shard ^ index
        return lax.dynamic_slice(partial, (away % 2, away // 2, 0, 0), (1, 1) + partial.shape[2:])[0, 0]

    partial = jnp.concatenate([of_shard(i) for i in range(shards)])
    rows_out = partial.shape[0] // sections
    result = lax.dynamic_slice_in_dim(partial, section * rows_out, rows_out, 0)
    for step in range(1, sections):
        sent = lax.dynamic_slice_in_dim(partial, (section ^ step) * rows_out, rows_out, 0)
        result = result + swap(sent, "section", step)
    return result


def sum_chips(value):
    chips = value.shape[0]
    rest = 1
    sent_as = value.dtype
    for digit in reversed(radices(chips)):
        steps = step_list(rest, digit)
        got = [swap(value.astype(sent_as), "shard", step) for step in steps]
        value = value.astype(F32)
        for step, other in zip(steps, got):
            value = value + jnp.stack([other[chip ^ (step // 2)] for chip in range(chips)]).astype(F32)
        rest = rest * digit
    return value


def solution(mesh):
    placed = (
        P("section", "shard", None),
        P("shard", None),
        P("shard"),
        P("section", None),
        P("section", "shard", None),
        P("section", None, "shard"),
        P("section", None, None),
        P("section", None, None),
        P("section", "shard", None),
    )
    return jax.shard_map(
        per_device, mesh=mesh, in_specs=placed, out_specs=P("section", "shard"), check_vma=False
    )
```

time: 327 us -> 251 us (0.77)
  waiting for transfers between devices: 271 us -> 70.3 us
  starting transfers between devices: 4.07 us -> 101 us
  Pallas kernels: 0 us -> 24.7 us
  blocking collectives: 21.4 us -> 0 us
  local copies, waits for them, and re-layouts: 4.42 us -> 23.5 us
  between operations: 13.5 us -> 0.94 us
  other arithmetic: 3.83 us -> 14.6 us
  matrix products: 8.57 us -> 14.6 us
    all_gather x2 -> x0, waiting for transfers between devices: 159 us -> none  [the longest x1 81.9 us: per_device(): lax.all_gather(value_local, 'shard', axis=0, tiled=True)]
    ppermute x3 -> x60, starting transfers between devices: 4.03 us -> 101 us  [the longest x48 66.6 us: swap(): lax.ppermute(value, axis, [(i, i ^ step) for i in range(lax.axis_size(axi...]
    ppermute x3 -> x60, waiting for transfers between devices: 111 us -> 70.3 us  [the longest x48 46.3 us: swap(): lax.ppermute(value, axis, [(i, i ^ step) for i in range(lax.axis_size(axi...]
    pallas_call x0 -> x12, Pallas kernels: none -> 24.7 us  [the longest x6 13.7 us: choose(): pl.pallas_call(choose_body, out_shape=jax.ShapeDtypeStruct(value.shape, v...]
    all_gather x1 -> x0, blocking collectives: 14 us -> none  [per_device(): gathered = lax.all_gather(features, 'shard', axis=0, tiled=True)]
    unnamed x10 -> x93, local copies, waits for them, and re-layouts: 0.02 us -> 10.8 us
    psum x1 -> x0, blocking collectives: 7.46 us -> none  [per_device(): score_total = lax.psum(partial_value, 'section')]
    dot_general x4 -> x10, matrix products: 8.57 us -> 14.6 us  [the longest x4 4.85 us: dot_t(): lax.dot_general(left, right, (((1,), (1,)), ((), ())), preferred_element_...]
  transfers between devices with their start and end apart: 5 -> 60, of which waited for: 5 -> 27; matrix products, arithmetic and copies ran while one was open for 3% -> 14% of each run, Pallas kernels for 0% -> 9%
where the time goes in v2:
time: 251 us; the launch traced here: 250 us
  starting transfers between devices  101 us (40%)
  waiting for transfers between devices  70.3 us (28%)
  Pallas kernels  24.7 us (10%)
  local copies, waits for them, and re-layouts  23.5 us (9%)
  other arithmetic  14.6 us (6%)
  matrix products  14.6 us (6%)
    ppermute x48, starting transfers between devices, swap(): lax.ppermute(value, axis, [(i, i ^ step) for i in range(lax.axis_size(axi...  66.6 us
    ppermute x48, waiting for transfers between devices, swap(): lax.ppermute(value, axis, [(i, i ^ step) for i in range(lax.axis_size(axi...  46.3 us
    ppermute x3, waiting for transfers between devices, per_device(): message_from.append(lax.ppermute(message(section ^ step), 'section', pairs))  24 us
    ppermute x3, starting transfers between devices, per_device(): message_from.append(lax.ppermute(message(section ^ step), 'section', pairs))  22.3 us
    pallas_call x6, Pallas kernels, choose(): pl.pallas_call(choose_body, out_shape=jax.ShapeDtypeStruct(value.shape, v...  13.7 us
    unnamed x93, local copies, waits for them, and re-layouts  10.8 us
    ppermute x6, starting transfers between devices, exchange(): lax.ppermute(value, 'section', [(i, i ^ step) for i in range(1, sections)...  10.1 us
    pallas_call x3, Pallas kernels, layer_step(): pl.pallas_call(lambda *refs: layer_body(False, *refs), out_shape=(jax.Sha...  9.17 us
  transfers between devices with their start and end apart: 60, of which 27 were waited for; matrix products, arithmetic and copies ran while one was open for 14% of the time, Pallas kernels for 9%

profile of v2, /device:TPU:0, one launch (start us, length us, event | category | flops | bytes accessed | tf_op | source)
XLA Modules:
  0.0 249.6 jit_solution(17378475000792173558)
XLA Ops:
  5.9 5.1 %collective-permute-start.4 = (bf16[1,1,32,1024]{3,2,1,0:T(8,128)(2,1)S(1)}, bf16[1,1,32,1024]{3,2,1,0:T(8,128)(2,1)S(1)}, u32[]{:S(2)}, u32[]{:S(2)}) collective-permute-start(bf16[1,1,32,1024]{3,2,1,0:T(8,128)(2,1)S(1)} %slice_bitcast_fusion.10), channel_id=1, source_target_pairs={{0,6},{1,7},{2,4},{3,5},{4,2},{5,3},{6,0},{7,1},{8,14},{9,15},{10,... | collective-permute-start | bytes 196616 | tf_op jit(solution)/shard_map/ppermute | solution.py:15
  14.2 2.3 collective-permute-done.3
  16.6 2.7 %collective-permute-start.11 = (bf16[1,1,96,1024]{3,2,1,0:T(8,128)(2,1)S(1)}, bf16[1,1,96,1024]{3,2,1,0:T(8,128)(2,1)S(1)}, u32[]{:S(2)}, u32[]{:S(2)}) collective-permute-start(bf16[1,1,96,1024]{3,2,1,0:T(8,128)(2,1)S(1)} %get-tuple-element.97), channel_id=1, source_target_pairs={{0,6},{1,7},{2,4},{3,5},{4,2},{5,3},{6,0},{7,1},{8,14},{9,15},{10,... | collective-permute-start | bytes 589832 | tf_op jit(solution)/shard_map/ppermute | solution.py:15
  19.4 6.8 %collective-permute-done.11 = bf16[1,1,96,1024]{3,2,1,0:T(8,128)(2,1)S(1)} collective-permute-done((bf16[1,1,96,1024]{3,2,1,0:T(8,128)(2,1)S(1)}, bf16[1,1,96,1024]{3,2,1,0:T(8,128)(2,1)S(1)}, u32[]{:S(2)}, u32[]{:S(2)}) %collective-permute-start.11) | collective-permute-done | bytes 196640 | tf_op jit(solution)/shard_map/ppermute | solution.py:15
  26.2 6.4 %collective-permute-start.9 = (bf16[1,1,96,1024]{3,2,1,0:T(8,128)(2,1)S(1)}, bf16[1,1,96,1024]{3,2,1,0:T(8,128)(2,1)S(1)}, u32[]{:S(2)}, u32[]{:S(2)}) collective-permute-start(bf16[1,1,96,1024]{3,2,1,0:T(8,128)(2,1)S(1)} %get-tuple-element.99), channel_id=1, source_target_pairs={{0,2},{1,3},{2,0},{3,1},{4,6},{5,7},{6,4},{7,5},{8,10},{9,11},{10,... | collective-permute-start | bytes 589832 | tf_op jit(solution)/shard_map/ppermute | solution.py:15
  33.6 2.4 collective-permute-done.10
  42.8 3.0 %fusion.7 = f32[384,1024]{1,0:T(8,128)} fusion(bf16[512,1024]{1,0:T(8,128)(2,1)} %fusion.refs_0_, bf16[384,1024]{1,0:T(8,128)(2,1)S(1)} %bitcast.186), kind=kOutput, calls=%fused_computation.18 | convolution fusion | flops 402653184 | bytes 3014656 | tf_op jit(solution)/shard_map/dot_general | solution.py:275
  50.5 2.5 %collective-permute-start.15 = (bf16[1,96,1024]{2,1,0:T(8,128)(2,1)S(1)}, bf16[1,96,1024]{2,1,0:T(8,128)(2,1)S(1)}, u32[]{:S(2)}, u32[]{:S(2)}) collective-permute-start(bf16[1,96,1024]{2,1,0:T(8,128)(2,1)S(1)} %get-tuple-element.92), channel_id=1, source_target_pairs={{0,6},{1,7},{2,4},{3,5},{4,2},{5,3},{6,0},{7,1},{8,14},{9,15},{10,... | collective-permute-start | bytes 589832 | tf_op jit(solution)/shard_map/ppermute | solution.py:15
  56.3 16.6 %collective-permute-start.23 = (bf16[192,1024]{1,0:T(8,128)(2,1)}, bf16[192,1024]{1,0:T(8,128)(2,1)}, u32[]{:S(2)}, u32[]{:S(2)}) collective-permute-start(bf16[192,1024]{1,0:T(8,128)(2,1)} %get-tuple-element.147), channel_id=1, source_target_pairs={{0,24},{8,16},{16,8},{1,25},{9,17},{17,9},{2,26},{10,18},{18,10},{... | collective-permute-start | bytes 1179656 | tf_op jit(solution)/shard_map/ppermute | solution.py:272
  73.0 3.7 %collective-permute-start.21 = (bf16[192,1024]{1,0:T(8,128)(2,1)}, bf16[192,1024]{1,0:T(8,128)(2,1)}, u32[]{:S(2)}, u32[]{:S(2)}) collective-permute-start(bf16[192,1024]{1,0:T(8,128)(2,1)} %get-tuple-element.148), channel_id=1, source_target_pairs={{0,8},{16,24},{24,16},{1,9},{17,25},{25,17},{2,10},{18,26},{26,18}... | collective-permute-start | bytes 1179656 | tf_op jit(solution)/shard_map/ppermute | solution.py:272
  90.1 23.7 %collective-permute-done.22 = bf16[192,1024]{1,0:T(8,128)(2,1)} collective-permute-done((bf16[192,1024]{1,0:T(8,128)(2,1)}, bf16[192,1024]{1,0:T(8,128)(2,1)}, u32[]{:S(2)}, u32[]{:S(2)}) %collective-permute-start.22) | collective-permute-done | bytes 393248 | tf_op jit(solution)/shard_map/ppermute | solution.py:272
  116.4 2.4 collective-permute-start.6
  128.5 2.3 shard_map.94.refs_8_
  134.5 4.0 %collective-permute-done.35 = f32[96,128]{0,1:T(8,128)S(1)} collective-permute-done((f32[96,128]{0,1:T(8,128)S(1)}, f32[96,128]{0,1:T(8,128)S(1)}, u32[]{:S(2)}, u32[]{:S(2)}) %collective-permute-start.35) | collective-permute-done | bytes 49184 | tf_op jit(solution)/shard_map/ppermute | solution.py:15
  145.8 2.3 shard_map.97.refs_6_
  154.0 3.1 %shard_map.95 = (f32[128,1024]{1,0:T(8,128)S(1)}, bf16[128,1024]{1,0:T(8,128)(2,1)S(1)}) custom-call(bf16[32,1152]{1,0:T(8,128)(2,1)S(1)} %shard_map.92.refs_0_, bf16[32,1152]{1,0:T(8,128)(2,1)S(1)} %collective-permute-done.24.refs_1_, bf16[32,1152]{1,0:T(8,128)(2,1)S(1)} %collective-permute-done.25.refs_2_, ...), custom_call_target="tpu_custom_call" | custom-call | flops 536870912 | bytes 5767168 | tf_op jit(solution)/shard_map/pallas_call | solution.py:180
  167.2 2.7 %collective-permute-done.31 = bf16[1,32,1024]{2,1,0:T(8,128)(2,1)S(1)} collective-permute-done((bf16[1,32,1024]{2,1,0:T(8,128)(2,1)S(1)}, bf16[1,32,1024]{2,1,0:T(8,128)(2,1)S(1)}, u32[]{:S(2)}, u32[]{:S(2)}) %collective-permute-start.31) | collective-permute-done | bytes 65568 | tf_op jit(solution)/shard_map/ppermute | solution.py:15
  172.1 2.5 %collective-permute-start.37 = (bf16[32,1152]{1,0:T(8,128)(2,1)S(1)}, bf16[32,1152]{1,0:T(8,128)(2,1)S(1)}, u32[]{:S(2)}, u32[]{:S(2)}) collective-permute-start(bf16[32,1152]{1,0:T(8,128)(2,1)S(1)} %shard_map.96.refs_0_), channel_id=1, source_target_pairs={{0,2},{1,3},{2,0},{3,1},{4,6},{5,7},{6,4},{7,5},{8,10},{9,11},{10,... | collective-permute-start | bytes 221192 | tf_op jit(solution)/shard_map/ppermute | solution.py:15
  179.2 3.1 %shard_map.99 = (f32[128,1024]{1,0:T(8,128)S(1)}, bf16[128,1024]{1,0:T(8,128)(2,1)S(1)}) custom-call(bf16[32,1152]{1,0:T(8,128)(2,1)S(1)} %shard_map.96.refs_0_, bf16[32,1152]{1,0:T(8,128)(2,1)S(1)} %collective-permute-done.37.refs_1_, bf16[32,1152]{1,0:T(8,128)(2,1)S(1)} %collective-permute-done.38.refs_2_, ...), custom_call_target="tpu_custom_call" | custom-call | flops 536870912 | bytes 5767168 | tf_op jit(solution)/shard_map/pallas_call | solution.py:180
  185.8 2.4 collective-permute-start.43
  197.6 2.4 collective-permute-start.46
  207.5 3.0 %shard_map.102 = (f32[128,1024]{1,0:T(8,128)}, f32[128,64]{1,0:T(8,128)S(1)}) custom-call(bf16[32,1152]{1,0:T(8,128)(2,1)S(1)} %shard_map.100.refs_0_, bf16[32,1152]{1,0:T(8,128)(2,1)} %collective-permute-done.46.refs_1_, bf16[32,1152]{1,0:T(8,128)(2,1)} %collective-permute-done.47.refs_2_, bf16[32,1152]{1,0:T(8,128)(2,1)S(1)} %collective-permute-done.48.refs_3_, ...), custom_call_target="tpu_custom_call" | custom-call | flops 285212672 | bytes 3801088 | tf_op jit(solution)/shard_map/pallas_call | solution.py:180
  224.8 6.4 %collective-permute-start.56 = (bf16[8,32,64]{1,2,0:T(8,128)(2,1)}, bf16[8,32,64]{1,2,0:T(8,128)(2,1)S(1)}, u32[]{:S(2)}, u32[]{:S(2)}) collective-permute-start(bf16[8,32,64]{1,2,0:T(8,128)(2,1)} %get-tuple-element.85), channel_id=1, source_target_pairs={{0,8},{8,0},{16,24},{24,16},{1,9},{9,1},{17,25},{25,17},{2,10},{10... | collective-permute-start | bytes 98312 | tf_op jit(solution)/shard_map/ppermute | solution.py:15
  235.3 3.3 %collective-permute-done.55 = bf16[8,32,64]{1,2,0:T(8,128)(2,1)S(1)} collective-permute-done((bf16[8,32,64]{1,2,0:T(8,128)(2,1)}, bf16[8,32,64]{1,2,0:T(8,128)(2,1)S(1)}, u32[]{:S(2)}, u32[]{:S(2)}) %collective-permute-start.55) | collective-permute-done | bytes 32800 | tf_op jit(solution)/shard_map/ppermute | solution.py:15
  (272 shorter events, 133.5 us)
Async XLA Ops:
  0.0 45.8 %collective-permute-start.1 = (bf16[1024,512]{1,0:T(8,128)(2,1)}, bf16[1024,512]{1,0:T(8,128)(2,1)}, u32[]{:S(2)}, u32[]{:S(2)}) collective-permute-start(bf16[1024,512]{1,0:T(8,128)(2,1)} %bitcast.180), channel_id=1, source_target_pairs={{8,24},{24,8},{9,25},{25,9},{10,26},{26,10},{11,27},{27,11},{12,28... | collective-permute-start | bytes 3145736 | tf_op jit(solution)/shard_map/ppermute | solution.py:80
  1.8 44.0 %collective-permute-start = (bf16[1024,512]{1,0:T(8,128)(2,1)}, bf16[1024,512]{1,0:T(8,128)(2,1)}, u32[]{:S(2)}, u32[]{:S(2)}) collective-permute-start(bf16[1024,512]{1,0:T(8,128)(2,1)} %bitcast.181), channel_id=1, source_target_pairs={{16,24},{24,16},{17,25},{25,17},{18,26},{26,18},{19,27},{27,19},{2... | collective-permute-start | bytes 3145736 | tf_op jit(solution)/shard_map/ppermute | solution.py:80
  13.9 34.2 %collective-permute-start.12 = (bf16[512,1024]{1,0:T(8,128)(2,1)}, bf16[512,1024]{1,0:T(8,128)(2,1)}, u32[]{:S(2)}, u32[]{:S(2)}) collective-permute-start(bf16[512,1024]{1,0:T(8,128)(2,1)} %fusion.refs_0_), channel_id=1, source_target_pairs={{0,1},{1,0},{2,3},{3,2},{4,5},{5,4},{6,7},{7,6},{8,9},{9,8},{10,11... | collective-permute-start | bytes 3145736 | tf_op jit(solution)/shard_map/ppermute | solution.py:15
  19.3 16.6 %collective-permute-start.10 = (bf16[1,1,96,1024]{3,2,1,0:T(8,128)(2,1)S(1)}, bf16[1,1,96,1024]{3,2,1,0:T(8,128)(2,1)S(1)}, u32[]{:S(2)}, u32[]{:S(2)}) collective-permute-start(bf16[1,1,96,1024]{3,2,1,0:T(8,128)(2,1)S(1)} %get-tuple-element.98), channel_id=1, source_target_pairs={{0,4},{1,5},{2,6},{3,7},{4,0},{5,1},{6,2},{7,3},{8,12},{9,13},{10,... | collective-permute-start | bytes 589832 | tf_op jit(solution)/shard_map/ppermute | solution.py:15
  26.2 13.8 %collective-permute-start.9 = (bf16[1,1,96,1024]{3,2,1,0:T(8,128)(2,1)S(1)}, bf16[1,1,96,1024]{3,2,1,0:T(8,128)(2,1)S(1)}, u32[]{:S(2)}, u32[]{:S(2)}) collective-permute-start(bf16[1,1,96,1024]{3,2,1,0:T(8,128)(2,1)S(1)} %get-tuple-element.99), channel_id=1, source_target_pairs={{0,2},{1,3},{2,0},{3,1},{4,6},{5,7},{6,4},{7,5},{8,10},{9,11},{10,... | collective-permute-start | bytes 589832 | tf_op jit(solution)/shard_map/ppermute | solution.py:15
  36.0 17.1 %collective-permute-start.17 = (bf16[512,1024]{1,0:T(8,128)(2,1)}, bf16[512,1024]{1,0:T(8,128)(2,1)}, u32[]{:S(2)}, u32[]{:S(2)}) collective-permute-start(bf16[512,1024]{1,0:T(8,128)(2,1)} %fusion.refs_0_), channel_id=1, source_target_pairs={{8,24},{24,8},{9,25},{25,9},{10,26},{26,10},{11,27},{27,11},{12,28... | collective-permute-start | bytes 3145736 | tf_op jit(solution)/shard_map/ppermute | solution.py:80
  40.1 16.3 %collective-permute-start.16 = (bf16[512,1024]{1,0:T(8,128)(2,1)}, bf16[512,1024]{1,0:T(8,128)(2,1)}, u32[]{:S(2)}, u32[]{:S(2)}) collective-permute-start(bf16[512,1024]{1,0:T(8,128)(2,1)} %fusion.refs_0_), channel_id=1, source_target_pairs={{16,24},{24,16},{17,25},{25,17},{18,26},{26,18},{19,27},{27,19},{2... | collective-permute-start | bytes 3145736 | tf_op jit(solution)/shard_map/ppermute | solution.py:80
  48.0 35.8 %collective-permute-start.5 = (bf16[1024,512]{1,0:T(8,128)(2,1)}, bf16[1024,512]{1,0:T(8,128)(2,1)}, u32[]{:S(2)}, u32[]{:S(2)}) collective-permute-start(bf16[1024,512]{1,0:T(8,128)(2,1)} %shard_map.91), channel_id=1, source_target_pairs={{0,1},{1,0},{2,3},{3,2},{4,5},{5,4},{6,7},{7,6},{8,9},{9,8},{10,11... | collective-permute-start | bytes 3145736 | tf_op jit(solution)/shard_map/ppermute | solution.py:15
  50.5 22.5 %collective-permute-start.15 = (bf16[1,96,1024]{2,1,0:T(8,128)(2,1)S(1)}, bf16[1,96,1024]{2,1,0:T(8,128)(2,1)S(1)}, u32[]{:S(2)}, u32[]{:S(2)}) collective-permute-start(bf16[1,96,1024]{2,1,0:T(8,128)(2,1)S(1)} %get-tuple-element.92), channel_id=1, source_target_pairs={{0,6},{1,7},{2,4},{3,5},{4,2},{5,3},{6,0},{7,1},{8,14},{9,15},{10,... | collective-permute-start | bytes 589832 | tf_op jit(solution)/shard_map/ppermute | solution.py:15
  53.0 23.6 %collective-permute-start.14 = (bf16[1,96,1024]{2,1,0:T(8,128)(2,1)S(1)}, bf16[1,96,1024]{2,1,0:T(8,128)(2,1)S(1)}, u32[]{:S(2)}, u32[]{:S(2)}) collective-permute-start(bf16[1,96,1024]{2,1,0:T(8,128)(2,1)S(1)} %get-tuple-element.93), channel_id=1, source_target_pairs={{0,4},{1,5},{2,6},{3,7},{4,0},{5,1},{6,2},{7,3},{8,12},{9,13},{10,... | collective-permute-start | bytes 589832 | tf_op jit(solution)/shard_map/ppermute | solution.py:15
  53.0 25.7 %collective-permute-start.13 = (bf16[1,96,1024]{2,1,0:T(8,128)(2,1)S(1)}, bf16[1,96,1024]{2,1,0:T(8,128)(2,1)S(1)}, u32[]{:S(2)}, u32[]{:S(2)}) collective-permute-start(bf16[1,96,1024]{2,1,0:T(8,128)(2,1)S(1)} %get-tuple-element.94), channel_id=1, source_target_pairs={{0,2},{1,3},{2,0},{3,1},{4,6},{5,7},{6,4},{7,5},{8,10},{9,11},{10,... | collective-permute-start | bytes 589832 | tf_op jit(solution)/shard_map/ppermute | solution.py:15
  56.3 31.3 %collective-permute-start.23 = (bf16[192,1024]{1,0:T(8,128)(2,1)}, bf16[192,1024]{1,0:T(8,128)(2,1)}, u32[]{:S(2)}, u32[]{:S(2)}) collective-permute-start(bf16[192,1024]{1,0:T(8,128)(2,1)} %get-tuple-element.147), channel_id=1, source_target_pairs={{0,24},{8,16},{16,8},{1,25},{9,17},{17,9},{2,26},{10,18},{18,10},{... | collective-permute-start | bytes 1179656 | tf_op jit(solution)/shard_map/ppermute | solution.py:272
  73.0 15.8 %collective-permute-start.21 = (bf16[192,1024]{1,0:T(8,128)(2,1)}, bf16[192,1024]{1,0:T(8,128)(2,1)}, u32[]{:S(2)}, u32[]{:S(2)}) collective-permute-start(bf16[192,1024]{1,0:T(8,128)(2,1)} %get-tuple-element.148), channel_id=1, source_target_pairs={{0,8},{16,24},{24,16},{1,9},{17,25},{25,17},{2,10},{18,26},{26,18}... | collective-permute-start | bytes 1179656 | tf_op jit(solution)/shard_map/ppermute | solution.py:272
  76.6 37.1 %collective-permute-start.22 = (bf16[192,1024]{1,0:T(8,128)(2,1)}, bf16[192,1024]{1,0:T(8,128)(2,1)}, u32[]{:S(2)}, u32[]{:S(2)}) collective-permute-start(bf16[192,1024]{1,0:T(8,128)(2,1)} %get-tuple-element.149), channel_id=1, source_target_pairs={{0,16},{8,24},{24,8},{1,17},{9,25},{25,9},{2,18},{10,26},{26,10},{... | collective-permute-start | bytes 1179656 | tf_op jit(solution)/shard_map/ppermute | solution.py:272
  83.1 32.0 %collective-permute-start.20 = (bf16[32,1152]{1,0:T(8,128)(2,1)S(1)}, bf16[32,1152]{1,0:T(8,128)(2,1)S(1)}, u32[]{:S(2)}, u32[]{:S(2)}) collective-permute-start(bf16[32,1152]{1,0:T(8,128)(2,1)S(1)} %get-tuple-element.140), channel_id=1, source_target_pairs={{8,16},{16,8},{9,17},{17,9},{10,18},{18,10},{11,19},{19,11},{12,20... | collective-permute-start | bytes 221192 | tf_op jit(solution)/shard_map/ppermute | solution.py:260
  83.8 44.6 %collective-permute-start.28 = (bf16[1024,512]{1,0:T(8,128)(2,1)S(1)}, bf16[1024,512]{1,0:T(8,128)(2,1)}, u32[]{:S(2)}, u32[]{:S(2)}) collective-permute-start(bf16[1024,512]{1,0:T(8,128)(2,1)S(1)} %bitcast.185), channel_id=1, source_target_pairs={{8,16},{16,8},{9,17},{17,9},{10,18},{18,10},{11,19},{19,11},{12,20... | collective-permute-start | bytes 3145736 | tf_op jit(solution)/shard_map/ppermute | solution.py:80
  87.7 27.4 %collective-permute-start.19 = (bf16[32,1152]{1,0:T(8,128)(2,1)S(1)}, bf16[32,1152]{1,0:T(8,128)(2,1)S(1)}, u32[]{:S(2)}, u32[]{:S(2)}) collective-permute-start(bf16[32,1152]{1,0:T(8,128)(2,1)S(1)} %get-tuple-element.141), channel_id=1, source_target_pairs={{8,24},{24,8},{9,25},{25,9},{10,26},{26,10},{11,27},{27,11},{12,28... | collective-permute-start | bytes 221192 | tf_op jit(solution)/shard_map/ppermute | solution.py:260
  88.7 30.0 %collective-permute-start.18 = (bf16[32,1152]{1,0:T(8,128)(2,1)}, bf16[32,1152]{1,0:T(8,128)(2,1)S(1)}, u32[]{:S(2)}, u32[]{:S(2)}) collective-permute-start(bf16[32,1152]{1,0:T(8,128)(2,1)} %get-tuple-element.142), channel_id=1, source_target_pairs={{16,24},{24,16},{17,25},{25,17},{18,26},{26,18},{19,27},{27,19},{2... | collective-permute-start | bytes 221192 | tf_op jit(solution)/shard_map/ppermute | solution.py:260
  122.7 22.0 %collective-permute-start.40 = (bf16[512,1024]{1,0:T(8,128)(2,1)}, bf16[512,1024]{1,0:T(8,128)(2,1)}, u32[]{:S(2)}, u32[]{:S(2)}) collective-permute-start(bf16[512,1024]{1,0:T(8,128)(2,1)} %fusion.refs_0_), channel_id=1, source_target_pairs={{8,16},{16,8},{9,17},{17,9},{10,18},{18,10},{11,19},{19,11},{12,20... | collective-permute-start | bytes 3145736 | tf_op jit(solution)/shard_map/ppermute | solution.py:80
  128.4 24.6 %collective-permute-start.27 = (bf16[512,1024]{1,0:T(8,128)(2,1)}, bf16[512,1024]{1,0:T(8,128)(2,1)}, u32[]{:S(2)}, u32[]{:S(2)}) collective-permute-start(bf16[512,1024]{1,0:T(8,128)(2,1)} %shard_map.93.refs_6_), channel_id=1, source_target_pairs={{0,1},{1,0},{2,3},{3,2},{4,5},{5,4},{6,7},{7,6},{8,9},{9,8},{10,11... | collective-permute-start | bytes 3145736 | tf_op jit(solution)/shard_map/ppermute | solution.py:15
  130.9 22.1 %collective-permute-start.29 = (bf16[1024,512]{1,0:T(8,128)(2,1)}, bf16[1024,512]{1,0:T(8,128)(2,1)}, u32[]{:S(2)}, u32[]{:S(2)}) collective-permute-start(bf16[1024,512]{1,0:T(8,128)(2,1)} %shard_map.94.refs_8_), channel_id=1, source_target_pairs={{0,1},{1,0},{2,3},{3,2},{4,5},{5,4},{6,7},{7,6},{8,9},{9,8},{10,11... | collective-permute-start | bytes 3145736 | tf_op jit(solution)/shard_map/ppermute | solution.py:15
  144.7 27.4 %collective-permute-start.42 = (bf16[1024,512]{1,0:T(8,128)(2,1)}, bf16[1024,512]{1,0:T(8,128)(2,1)}, u32[]{:S(2)}, u32[]{:S(2)}) collective-permute-start(bf16[1024,512]{1,0:T(8,128)(2,1)} %shard_map.98.refs_8_), channel_id=1, source_target_pairs={{0,1},{1,0},{2,3},{3,2},{4,5},{5,4},{6,7},{7,6},{8,9},{9,8},{10,11... | collective-permute-start | bytes 3145736 | tf_op jit(solution)/shard_map/ppermute | solution.py:15
  150.4 28.7 %collective-permute-start.41 = (bf16[512,1024]{1,0:T(8,128)(2,1)}, bf16[512,1024]{1,0:T(8,128)(2,1)}, u32[]{:S(2)}, u32[]{:S(2)}) collective-permute-start(bf16[512,1024]{1,0:T(8,128)(2,1)} %shard_map.97.refs_6_), channel_id=1, source_target_pairs={{0,1},{1,0},{2,3},{3,2},{4,5},{5,4},{6,7},{7,6},{8,9},{9,8},{10,11... | collective-permute-start | bytes 3145736 | tf_op jit(solution)/shard_map/ppermute | solution.py:15
  163.0 40.3 %collective-permute-start.49 = (bf16[512,1024]{1,0:T(8,128)(2,1)}, bf16[512,1024]{1,0:T(8,128)(2,1)}, u32[]{:S(2)}, u32[]{:S(2)}) collective-permute-start(bf16[512,1024]{1,0:T(8,128)(2,1)} %shard_map.101.refs_6_), channel_id=1, source_target_pairs={{0,1},{1,0},{2,3},{3,2},{4,5},{5,4},{6,7},{7,6},{8,9},{9,8},{10,11... | collective-permute-start | bytes 3145736 | tf_op jit(solution)/shard_map/ppermute | solution.py:15
  (81 other events, 856.1 us)

commit v3 on v2

--- a/solution.py
+++ b/solution.py
@@ -260,16 +260,8 @@
             out[step] = lax.ppermute(part(section ^ step), "section", pairs)
         return out
 
+    columns_from = to_groups(columns_padded, 1)
     proj_piece = chip_columns(grad_proj[0].T, 0)
-
-    def message(other):
-        part = lax.dynamic_slice_in_dim(columns_padded, jnp.maximum(other - 1, 0) * rows, rows, 1)
-        return jnp.concatenate([part.reshape(block, 2 * columns), proj_piece])
-
-    message_from = [message(section)]
-    for step in range(1, sections):
-        pairs = [(i, i ^ step) for i in range(sections) if i ^ step > 0]
-        message_from.append(lax.ppermute(message(section ^ step), "section", pairs))
 
     flat = hidden_columns.reshape(chips * tokens, 2 * columns)
     part = jnp.dot(flat[:, :columns], value_scaled, preferred_element_type=F32)
@@ -295,16 +287,9 @@
         axis=1,
     )
 
-    value_rows, own_output = lax.optimization_barrier((value_rows, output_weight[0]))
+    value_rows, own_output, columns_from = lax.optimization_barrier((value_rows, output_weight[0], columns_from))
     value_rows_from = to_groups(jnp.pad(value_rows, ((0, padded - tokens), (0, 0))), 0)
     far_output = exchange(own_output, far, sections)
-
-    def message_of(layer):
-        distance = layer ^ section
-        result = message_from[0]
-        for step in range(1, sections):
-            result = jnp.where(distance == step, message_from[step], result)
-        return result
 
     output_near = choose(output_from, sections - 1, section, sections)
     output_far = swap(output_near, "shard", 1)
@@ -317,28 +302,35 @@
         if layer == max(sections - 2, 1) and sections > 2:
             terms, mine = lax.optimization_barrier((terms, mine))
         if layer == sections - 1:
-            terms, value_rows_from, message_from, own_value = lax.optimization_barrier(
-                (terms, value_rows_from, message_from, value_scaled)
-            )
-            output_from.update(far_output)
+            terms, value_rows_from, own_value = lax.optimization_barrier((terms, value_rows_from, value_scaled))
             value_from.update(exchange(own_value, far, sections))
-            messages = [message_of(place) for place in range(sections)]
+
+        def proj_of(place):
+            result = proj_from[0]
+            for step in range(1, sections):
+                result = jnp.where((place ^ section) == step, proj_from[step], result)
+            return result
+
         act = pick(value_rows_from, layer, section, sections)
         pieces = gather_pieces(rows_step(terms, act, width))
+        if layer == sections - 1:
+            pieces, far_output = lax.optimization_barrier((pieces, far_output))
+            output_from.update(far_output)
         value_near = choose(value_from, layer, section, sections)
         value_far = swap(value_near, "shard", 1)
         if layer < sections - 1:
-            low_parts.append(dot_t(state.astype(BF16), messages[layer][block:]))
+            low_parts.append(dot_t(state.astype(BF16), proj_of(layer)))
         if layer > 1:
             next_near = choose(output_from, layer - 1, section, sections)
             next_far = swap(next_near, "shard", 1)
         else:
-            next_near = messages[0][block:, :columns]
-            next_far = messages[0][block:, columns:]
+            first = proj_of(0)
+            next_near = first[:, :columns]
+            next_far = first[:, columns:]
         state, part = layer_step(
             pieces,
             state,
-            messages[layer][:block],
+            pick(columns_from, layer, section, sections).reshape(block, 2 * columns),
             value_near,
             value_far,
             next_near,
@@ -346,7 +338,15 @@
             BF16 if layer > 1 else F32,
         )
         if layer == sections - 1:
-            mine = gather_chips(jnp.concatenate([value_low, grad_low_top], axis=1))
+            mine = jnp.concatenate([value_low, grad_low_top], axis=1)
+            state, part, mine, proj_piece, value_from, output_from = lax.optimization_barrier(
+                (state, part, mine, proj_piece, value_from, output_from)
+            )
+            proj_from = [proj_piece]
+            for step in range(1, sections):
+                pairs = [(i, i ^ step) for i in range(sections - 1) if i ^ step > 0]
+                proj_from.append(lax.ppermute(proj_piece, "section", pairs))
+            mine = gather_chips(mine)
             mine = jnp.concatenate([mine, swap(mine, "shard", 1)])
     low_parts.append(part)
     low = jnp.concatenate(low_parts, axis=1).astype(BF16)

time: 251 us -> 280 us (1.12)
  starting transfers between devices: 101 us -> 134 us
  waiting for transfers between devices: 70.3 us -> 54.4 us
  local copies, waits for them, and re-layouts: 23.5 us -> 32.9 us
  other arithmetic: 14.6 us -> 17.9 us
    ppermute x3, starting transfers between devices: 22.3 us -> 52.9 us  [per_device(): proj_from.append(lax.ppermute(proj_piece, 'section', pairs))]
    ppermute x3, waiting for transfers between devices: 24 us -> 0.01 us  [per_device(): proj_from.append(lax.ppermute(proj_piece, 'section', pairs))]
    ppermute x48, waiting for transfers between devices: 46.3 us -> 54.4 us  [swap(): lax.ppermute(value, axis, [(i, i ^ step) for i in range(lax.axis_size(axi...]
    ppermute x3 -> x6, starting transfers between devices: 1.97 us -> 6.1 us  [to_groups(): out[step] = lax.ppermute(part(section ^ step), 'section', pairs)]
    unnamed x93 -> x103, local copies, waits for them, and re-layouts: 10.8 us -> 14.7 us
    select_n x1 -> x2, other arithmetic: 0.04 us -> 2.92 us  [pick(): result = jnp.where(distance == key, values[key], result)]
  transfers between devices with their start and end apart: 60 -> 63, of which waited for: 27 -> 22; matrix products, arithmetic and copies ran while one was open for 14% -> 16% of each run, Pallas kernels for 9% -> 7%
where the time goes in v3:
time: 280 us; the launch traced here: 278 us
  starting transfers between devices  134 us (48%)
  waiting for transfers between devices  54.4 us (19%)
  local copies, waits for them, and re-layouts  32.9 us (12%)
  Pallas kernels  23.6 us (8%)
  other arithmetic  17.9 us (6%)
  matrix products  14.5 us (5%)
    ppermute x48, starting transfers between devices, swap(): lax.ppermute(value, axis, [(i, i ^ step) for i in range(lax.axis_size(axi...  64.5 us
    ppermute x48, waiting for transfers between devices, swap(): lax.ppermute(value, axis, [(i, i ^ step) for i in range(lax.axis_size(axi...  54.4 us
    ppermute x3, starting transfers between devices, per_device(): proj_from.append(lax.ppermute(proj_piece, 'section', pairs))  52.9 us
    unnamed x103, local copies, waits for them, and re-layouts  14.7 us
    pallas_call x6, Pallas kernels, choose(): pl.pallas_call(choose_body, out_shape=jax.ShapeDtypeStruct(value.shape, v...  13.3 us
    ppermute x6, starting transfers between devices, exchange(): lax.ppermute(value, 'section', [(i, i ^ step) for i in range(1, sections)...  10 us
    pallas_call x3, Pallas kernels, layer_step(): pl.pallas_call(lambda *refs: layer_body(False, *refs), out_shape=(jax.Sha...  8.5 us
    ppermute x6, starting transfers between devices, to_groups(): out[step] = lax.ppermute(part(section ^ step), 'section', pairs)  6.1 us
  transfers between devices with their start and end apart: 63, of which 22 were waited for; matrix products, arithmetic and copies ran while one was open for 16% of the time, Pallas kernels for 7%

profile of v3, /device:TPU:0, one launch (start us, length us, event | category | flops | bytes accessed | tf_op | source)
XLA Modules:
  0.0 277.8 jit_solution(11226001329193580663)
XLA Ops:
  7.9 3.9 %collective-permute-start.3 = (bf16[1,1,32,1024]{3,2,1,0:T(8,128)(2,1)S(1)}, bf16[1,1,32,1024]{3,2,1,0:T(8,128)(2,1)S(1)}, u32[]{:S(2)}, u32[]{:S(2)}) collective-permute-start(bf16[1,1,32,1024]{3,2,1,0:T(8,128)(2,1)S(1)} %get-tuple-element.167), channel_id=1, source_target_pairs={{0,4},{1,5},{2,6},{3,7},{4,0},{5,1},{6,2},{7,3},{8,12},{9,13},{10,... | collective-permute-start | bytes 196616 | tf_op jit(solution)/shard_map/ppermute | solution.py:15
  16.6 2.7 collective-permute-start.4
  20.0 5.7 %collective-permute-done.4 = bf16[1,1,32,1024]{3,2,1,0:T(8,128)(2,1)S(1)} collective-permute-done((bf16[1,1,32,1024]{3,2,1,0:T(8,128)(2,1)S(1)}, bf16[1,1,32,1024]{3,2,1,0:T(8,128)(2,1)S(1)}, u32[]{:S(2)}, u32[]{:S(2)}) %collective-permute-start.4) | collective-permute-done | bytes 65568 | tf_op jit(solution)/shard_map/ppermute | solution.py:15
  28.5 10.6 %collective-permute-done.10 = bf16[1,1,96,1024]{3,2,1,0:T(8,128)(2,1)} collective-permute-done((bf16[1,1,96,1024]{3,2,1,0:T(8,128)(2,1)}, bf16[1,1,96,1024]{3,2,1,0:T(8,128)(2,1)}, u32[]{:S(2)}, u32[]{:S(2)}) %collective-permute-start.10) | collective-permute-done | bytes 196640 | tf_op jit(solution)/shard_map/ppermute | solution.py:15
  47.8 2.4 add_convert_fusion
  51.2 3.1 %collective-permute-start.13 = (bf16[1,96,1024]{2,1,0:T(8,128)(2,1)}, bf16[1,96,1024]{2,1,0:T(8,128)(2,1)}, u32[]{:S(2)}, u32[]{:S(2)}) collective-permute-start(bf16[1,96,1024]{2,1,0:T(8,128)(2,1)} %get-tuple-element.123), channel_id=1, source_target_pairs={{0,2},{1,3},{2,0},{3,1},{4,6},{5,7},{6,4},{7,5},{8,10},{9,11},{10,... | collective-permute-start | bytes 589832 | tf_op jit(solution)/shard_map/ppermute | solution.py:15
  61.0 3.3 %collective-permute-done.13 = bf16[1,96,1024]{2,1,0:T(8,128)(2,1)} collective-permute-done((bf16[1,96,1024]{2,1,0:T(8,128)(2,1)}, bf16[1,96,1024]{2,1,0:T(8,128)(2,1)}, u32[]{:S(2)}, u32[]{:S(2)}) %collective-permute-start.13) | collective-permute-done | bytes 196640 | tf_op jit(solution)/shard_map/ppermute | solution.py:15
  65.7 3.7 %collective-permute-start.15 = (bf16[1,96,1024]{2,1,0:T(8,128)(2,1)S(1)}, bf16[1,96,1024]{2,1,0:T(8,128)(2,1)S(1)}, u32[]{:S(2)}, u32[]{:S(2)}) collective-permute-start(bf16[1,96,1024]{2,1,0:T(8,128)(2,1)S(1)} %copy-done.40), channel_id=1, source_target_pairs={{0,6},{1,7},{2,4},{3,5},{4,2},{5,3},{6,0},{7,1},{8,14},{9,15},{10,... | collective-permute-start | bytes 589832 | tf_op jit(solution)/shard_map/ppermute | solution.py:15
  69.4 4.9 %collective-permute-done.15 = bf16[1,96,1024]{2,1,0:T(8,128)(2,1)S(1)} collective-permute-done((bf16[1,96,1024]{2,1,0:T(8,128)(2,1)S(1)}, bf16[1,96,1024]{2,1,0:T(8,128)(2,1)S(1)}, u32[]{:S(2)}, u32[]{:S(2)}) %collective-permute-start.15) | collective-permute-done | bytes 196640 | tf_op jit(solution)/shard_map/ppermute | solution.py:15
  85.7 3.7 %collective-permute-start.6 = (bf16[1,32,1024]{2,1,0:T(8,128)(2,1)S(1)}, bf16[1,32,1024]{2,1,0:T(8,128)(2,1)S(1)}, u32[]{:S(2)}, u32[]{:S(2)}) collective-permute-start(bf16[1,32,1024]{2,1,0:T(8,128)(2,1)S(1)} %get-tuple-element.164), channel_id=1, source_target_pairs={{0,2},{1,3},{2,0},{3,1},{4,6},{5,7},{6,4},{7,5},{8,10},{9,11},{10,... | collective-permute-start | bytes 196616 | tf_op jit(solution)/shard_map/ppermute | solution.py:15
  92.5 3.1 %collective-permute-done.7 = bf16[1,32,1024]{2,1,0:T(8,128)(2,1)S(1)} collective-permute-done((bf16[1,32,1024]{2,1,0:T(8,128)(2,1)S(1)}, bf16[1,32,1024]{2,1,0:T(8,128)(2,1)S(1)}, u32[]{:S(2)}, u32[]{:S(2)}) %collective-permute-start.7) | collective-permute-done | bytes 65568 | tf_op jit(solution)/shard_map/ppermute | solution.py:15
  117.9 2.4 shard_map.95
  136.8 3.0 %collective-permute-done.31 = bf16[1,32,1024]{2,1,0:T(8,128)(2,1)S(1)} collective-permute-done((bf16[1,32,1024]{2,1,0:T(8,128)(2,1)S(1)}, bf16[1,32,1024]{2,1,0:T(8,128)(2,1)S(1)}, u32[]{:S(2)}, u32[]{:S(2)}) %collective-permute-start.31) | collective-permute-done | bytes 65568 | tf_op jit(solution)/shard_map/ppermute | solution.py:15
  141.9 36.3 %collective-permute-start.38 = (bf16[64,1024]{1,0:T(8,128)(2,1)}, bf16[64,1024]{1,0:T(8,128)(2,1)}, u32[]{:S(2)}, u32[]{:S(2)}) collective-permute-start(bf16[64,1024]{1,0:T(8,128)(2,1)} %pad_maximum_fusion.8), channel_id=1, source_target_pairs={{0,24},{8,16},{16,8},{1,25},{9,17},{17,9},{2,26},{10,18},{18,10},{... | collective-permute-start | bytes 393224 | tf_op jit(solution)/shard_map/ppermute | solution.py:348
  178.8 13.6 %collective-permute-start.39 = (bf16[64,1024]{1,0:T(8,128)(2,1)}, bf16[64,1024]{1,0:T(8,128)(2,1)}, u32[]{:S(2)}, u32[]{:S(2)}) collective-permute-start(bf16[64,1024]{1,0:T(8,128)(2,1)} %pad_maximum_fusion.8), channel_id=1, source_target_pairs={{0,16},{8,24},{1,17},{9,25},{2,18},{10,26},{3,19},{11,27},{4,20},{... | collective-permute-start | bytes 393224 | tf_op jit(solution)/shard_map/ppermute | solution.py:348
  192.4 3.1 %collective-permute-start.40 = (bf16[64,1024]{1,0:T(8,128)(2,1)}, bf16[64,1024]{1,0:T(8,128)(2,1)}, u32[]{:S(2)}, u32[]{:S(2)}) collective-permute-start(bf16[64,1024]{1,0:T(8,128)(2,1)} %pad_maximum_fusion.8), channel_id=1, source_target_pairs={{0,8},{16,24},{1,9},{17,25},{2,10},{18,26},{3,11},{19,27},{4,12},{... | collective-permute-start | bytes 393224 | tf_op jit(solution)/shard_map/ppermute | solution.py:348
  203.7 3.2 %collective-permute-start.42 = (bf16[32,1152]{1,0:T(8,128)(2,1)S(1)}, bf16[32,1152]{1,0:T(8,128)(2,1)S(1)}, u32[]{:S(2)}, u32[]{:S(2)}) collective-permute-start(bf16[32,1152]{1,0:T(8,128)(2,1)S(1)} %shard_map.96.refs_0_), channel_id=1, source_target_pairs={{0,4},{1,5},{2,6},{3,7},{4,0},{5,1},{6,2},{7,3},{8,12},{9,13},{10,... | collective-permute-start | bytes 221192 | tf_op jit(solution)/shard_map/ppermute | solution.py:15
  210.1 3.0 %collective-permute-done.42.refs_2_ = bf16[32,1152]{1,0:T(8,128)(2,1)S(1)} collective-permute-done((bf16[32,1152]{1,0:T(8,128)(2,1)S(1)}, bf16[32,1152]{1,0:T(8,128)(2,1)S(1)}, u32[]{:S(2)}, u32[]{:S(2)}) %collective-permute-start.42) | collective-permute-done | bytes 73760 | tf_op jit(solution)/shard_map/ppermute | solution.py:15
  213.2 3.1 %shard_map.99 = (f32[128,1024]{1,0:T(8,128)S(1)}, bf16[128,1024]{1,0:T(8,128)(2,1)S(1)}) custom-call(bf16[32,1152]{1,0:T(8,128)(2,1)S(1)} %shard_map.96.refs_0_, bf16[32,1152]{1,0:T(8,128)(2,1)S(1)} %collective-permute-done.41.refs_1_, bf16[32,1152]{1,0:T(8,128)(2,1)S(1)} %collective-permute-done.42.refs_2_, ...), custom_call_target="tpu_custom_call" | custom-call | flops 536870912 | bytes 5767168 | tf_op jit(solution)/shard_map/pallas_call | solution.py:180
  224.9 2.6 collective-permute-done.47
  242.1 3.0 %shard_map.102 = (f32[128,1024]{1,0:T(8,128)}, f32[128,64]{1,0:T(8,128)S(1)}) custom-call(bf16[32,1152]{1,0:T(8,128)(2,1)S(1)} %shard_map.100.refs_0_, bf16[32,1152]{1,0:T(8,128)(2,1)S(1)} %collective-permute-done.49.refs_1_, bf16[32,1152]{1,0:T(8,128)(2,1)} %collective-permute-done.50.refs_2_, bf16[32,1152]{1,0:T(8,128)(2,1)} %collective-permute-done.51.refs_3_, ...), custom_call_target="tpu_custom_call" | custom-call | flops 285212672 | bytes 3801088 | tf_op jit(solution)/shard_map/pallas_call | solution.py:180
  249.0 2.9 %collective-permute-done.54 = bf16[4,32,192]{2,1,0:T(8,128)(2,1)S(1)} collective-permute-done((bf16[4,32,192]{2,1,0:T(8,128)(2,1)S(1)}, bf16[4,32,192]{2,1,0:T(8,128)(2,1)S(1)}, u32[]{:S(2)}, u32[]{:S(2)}) %collective-permute-start.54) | collective-permute-done | bytes 49184 | tf_op jit(solution)/shard_map/ppermute | solution.py:15
  259.4 3.5 %collective-permute-start.59 = (bf16[8,32,64]{1,2,0:T(8,128)(2,1)}, bf16[8,32,64]{1,2,0:T(8,128)(2,1)S(1)}, u32[]{:S(2)}, u32[]{:S(2)}) collective-permute-start(bf16[8,32,64]{1,2,0:T(8,128)(2,1)} %get-tuple-element.114), channel_id=1, source_target_pairs={{0,8},{8,0},{16,24},{24,16},{1,9},{9,1},{17,25},{25,17},{2,10},{10... | collective-permute-start | bytes 98312 | tf_op jit(solution)/shard_map/ppermute | solution.py:15
  262.9 4.0 %collective-permute-done.57 = bf16[8,32,64]{1,2,0:T(8,128)(2,1)S(1)} collective-permute-done((bf16[8,32,64]{1,2,0:T(8,128)(2,1)}, bf16[8,32,64]{1,2,0:T(8,128)(2,1)S(1)}, u32[]{:S(2)}, u32[]{:S(2)}) %collective-permute-start.57) | collective-permute-done | bytes 32800 | tf_op jit(solution)/shard_map/ppermute | solution.py:15
  (287 shorter events, 146.0 us)
Async XLA Ops:
  0.0 45.5 %collective-permute-start = (bf16[1024,512]{1,0:T(8,128)(2,1)}, bf16[1024,512]{1,0:T(8,128)(2,1)}, u32[]{:S(2)}, u32[]{:S(2)}) collective-permute-start(bf16[1024,512]{1,0:T(8,128)(2,1)} %bitcast.187), channel_id=1, source_target_pairs={{16,24},{24,16},{17,25},{25,17},{18,26},{26,18},{19,27},{27,19},{2... | collective-permute-start | bytes 3145736 | tf_op jit(solution)/shard_map/ppermute | solution.py:80
  1.8 43.7 %collective-permute-start.1 = (bf16[1024,512]{1,0:T(8,128)(2,1)}, bf16[1024,512]{1,0:T(8,128)(2,1)}, u32[]{:S(2)}, u32[]{:S(2)}) collective-permute-start(bf16[1024,512]{1,0:T(8,128)(2,1)} %bitcast.188), channel_id=1, source_target_pairs={{8,24},{24,8},{9,25},{25,9},{10,26},{26,10},{11,27},{27,11},{12,28... | collective-permute-start | bytes 3145736 | tf_op jit(solution)/shard_map/ppermute | solution.py:80
  5.6 42.2 %collective-permute-start.12 = (bf16[512,1024]{1,0:T(8,128)(2,1)S(1)}, bf16[512,1024]{1,0:T(8,128)(2,1)}, u32[]{:S(2)}, u32[]{:S(2)}) collective-permute-start(bf16[512,1024]{1,0:T(8,128)(2,1)S(1)} %fusion.refs_0_), channel_id=1, source_target_pairs={{0,1},{1,0},{2,3},{3,2},{4,5},{5,4},{6,7},{7,6},{8,9},{9,8},{10,11... | collective-permute-start | bytes 3145736 | tf_op jit(solution)/shard_map/ppermute | solution.py:15
  15.4 10.4 %collective-permute-start.9 = (bf16[1,1,96,1024]{3,2,1,0:T(8,128)(2,1)S(1)}, bf16[1,1,96,1024]{3,2,1,0:T(8,128)(2,1)S(1)}, u32[]{:S(2)}, u32[]{:S(2)}) collective-permute-start(bf16[1,1,96,1024]{3,2,1,0:T(8,128)(2,1)S(1)} %get-tuple-element.127), channel_id=1, source_target_pairs={{0,2},{1,3},{2,0},{3,1},{4,6},{5,7},{6,4},{7,5},{8,10},{9,11},{10,... | collective-permute-start | bytes 589832 | tf_op jit(solution)/shard_map/ppermute | solution.py:15
  25.8 13.4 %collective-permute-start.10 = (bf16[1,1,96,1024]{3,2,1,0:T(8,128)(2,1)}, bf16[1,1,96,1024]{3,2,1,0:T(8,128)(2,1)}, u32[]{:S(2)}, u32[]{:S(2)}) collective-permute-start(bf16[1,1,96,1024]{3,2,1,0:T(8,128)(2,1)} %get-tuple-element.126), channel_id=1, source_target_pairs={{0,4},{1,5},{2,6},{3,7},{4,0},{5,1},{6,2},{7,3},{8,12},{9,13},{10,... | collective-permute-start | bytes 589832 | tf_op jit(solution)/shard_map/ppermute | solution.py:15
  26.4 14.4 %collective-permute-start.11 = (bf16[1,1,96,1024]{3,2,1,0:T(8,128)(2,1)}, bf16[1,1,96,1024]{3,2,1,0:T(8,128)(2,1)}, u32[]{:S(2)}, u32[]{:S(2)}) collective-permute-start(bf16[1,1,96,1024]{3,2,1,0:T(8,128)(2,1)} %slice_bitcast_fusion.3), channel_id=1, source_target_pairs={{0,6},{1,7},{2,4},{3,5},{4,2},{5,3},{6,0},{7,1},{8,14},{9,15},{10,... | collective-permute-start | bytes 589832 | tf_op jit(solution)/shard_map/ppermute | solution.py:15
  39.1 19.2 %collective-permute-start.16 = (bf16[512,1024]{1,0:T(8,128)(2,1)S(1)}, bf16[512,1024]{1,0:T(8,128)(2,1)}, u32[]{:S(2)}, u32[]{:S(2)}) collective-permute-start(bf16[512,1024]{1,0:T(8,128)(2,1)S(1)} %fusion.refs_0_), channel_id=1, source_target_pairs={{16,24},{24,16},{17,25},{25,17},{18,26},{26,18},{19,27},{27,19},{2... | collective-permute-start | bytes 3145736 | tf_op jit(solution)/shard_map/ppermute | solution.py:80
  40.8 18.9 %collective-permute-start.17 = (bf16[512,1024]{1,0:T(8,128)(2,1)S(1)}, bf16[512,1024]{1,0:T(8,128)(2,1)}, u32[]{:S(2)}, u32[]{:S(2)}) collective-permute-start(bf16[512,1024]{1,0:T(8,128)(2,1)S(1)} %fusion.refs_0_), channel_id=1, source_target_pairs={{8,24},{24,8},{9,25},{25,9},{10,26},{26,10},{11,27},{27,11},{12,28... | collective-permute-start | bytes 3145736 | tf_op jit(solution)/shard_map/ppermute | solution.py:80
  47.7 35.7 %collective-permute-start.5 = (bf16[1024,512]{1,0:T(8,128)(2,1)}, bf16[1024,512]{1,0:T(8,128)(2,1)}, u32[]{:S(2)}, u32[]{:S(2)}) collective-permute-start(bf16[1024,512]{1,0:T(8,128)(2,1)} %shard_map.91), channel_id=1, source_target_pairs={{0,1},{1,0},{2,3},{3,2},{4,5},{5,4},{6,7},{7,6},{8,9},{9,8},{10,11... | collective-permute-start | bytes 3145736 | tf_op jit(solution)/shard_map/ppermute | solution.py:15
  51.2 13.1 %collective-permute-start.13 = (bf16[1,96,1024]{2,1,0:T(8,128)(2,1)}, bf16[1,96,1024]{2,1,0:T(8,128)(2,1)}, u32[]{:S(2)}, u32[]{:S(2)}) collective-permute-start(bf16[1,96,1024]{2,1,0:T(8,128)(2,1)} %get-tuple-element.123), channel_id=1, source_target_pairs={{0,2},{1,3},{2,0},{3,1},{4,6},{5,7},{6,4},{7,5},{8,10},{9,11},{10,... | collective-permute-start | bytes 589832 | tf_op jit(solution)/shard_map/ppermute | solution.py:15
  54.3 11.5 %collective-permute-start.14 = (bf16[1,96,1024]{2,1,0:T(8,128)(2,1)}, bf16[1,96,1024]{2,1,0:T(8,128)(2,1)}, u32[]{:S(2)}, u32[]{:S(2)}) collective-permute-start(bf16[1,96,1024]{2,1,0:T(8,128)(2,1)} %get-tuple-element.122), channel_id=1, source_target_pairs={{0,4},{1,5},{2,6},{3,7},{4,0},{5,1},{6,2},{7,3},{8,12},{9,13},{10,... | collective-permute-start | bytes 589832 | tf_op jit(solution)/shard_map/ppermute | solution.py:15
  58.3 19.8 %collective-permute-start.18 = (bf16[4,32,1024]{2,1,0:T(8,128)(2,1)}, bf16[4,32,1024]{2,1,0:T(8,128)(2,1)}, u32[]{:S(2)}, u32[]{:S(2)}) collective-permute-start(bf16[4,32,1024]{2,1,0:T(8,128)(2,1)} %get-tuple-element.119), channel_id=1, source_target_pairs={{16,24},{24,16},{17,25},{25,17},{18,26},{26,18},{19,27},{27,19},{2... | collective-permute-start | bytes 786440 | tf_op jit(solution)/shard_map/ppermute | solution.py:260
  59.7 18.5 %collective-permute-start.19 = (bf16[4,32,1024]{2,1,0:T(8,128)(2,1)}, bf16[4,32,1024]{2,1,0:T(8,128)(2,1)}, u32[]{:S(2)}, u32[]{:S(2)}) collective-permute-start(bf16[4,32,1024]{2,1,0:T(8,128)(2,1)} %get-tuple-element.118), channel_id=1, source_target_pairs={{8,24},{24,8},{9,25},{25,9},{10,26},{26,10},{11,27},{27,11},{12,28... | collective-permute-start | bytes 786440 | tf_op jit(solution)/shard_map/ppermute | solution.py:260
  64.3 13.8 %collective-permute-start.20 = (bf16[4,32,1024]{2,1,0:T(8,128)(2,1)}, bf16[4,32,1024]{2,1,0:T(8,128)(2,1)}, u32[]{:S(2)}, u32[]{:S(2)}) collective-permute-start(bf16[4,32,1024]{2,1,0:T(8,128)(2,1)} %get-tuple-element.117), channel_id=1, source_target_pairs={{8,16},{16,8},{9,17},{17,9},{10,18},{18,10},{11,19},{19,11},{12,20... | collective-permute-start | bytes 786440 | tf_op jit(solution)/shard_map/ppermute | solution.py:260
  78.2 28.8 %collective-permute-start.27 = (bf16[1024,512]{1,0:T(8,128)(2,1)}, bf16[1024,512]{1,0:T(8,128)(2,1)}, u32[]{:S(2)}, u32[]{:S(2)}) collective-permute-start(bf16[1024,512]{1,0:T(8,128)(2,1)} %bitcast.190), channel_id=1, source_target_pairs={{8,16},{16,8},{9,17},{17,9},{10,18},{18,10},{11,19},{19,11},{12,20... | collective-permute-start | bytes 3145736 | tf_op jit(solution)/shard_map/ppermute | solution.py:80
  104.8 10.8 %collective-permute-start.28 = (bf16[512,1024]{1,0:T(8,128)(2,1)}, bf16[512,1024]{1,0:T(8,128)(2,1)S(1)}, u32[]{:S(2)}, u32[]{:S(2)}) collective-permute-start(bf16[512,1024]{1,0:T(8,128)(2,1)} %shard_map.93.refs_6_), channel_id=1, source_target_pairs={{0,1},{1,0},{2,3},{3,2},{4,5},{5,4},{6,7},{7,6},{8,9},{9,8},{10,11... | collective-permute-start | bytes 3145736 | tf_op jit(solution)/shard_map/ppermute | solution.py:15
  104.9 15.5 %collective-permute-start.30 = (bf16[512,1024]{1,0:T(8,128)(2,1)}, bf16[512,1024]{1,0:T(8,128)(2,1)}, u32[]{:S(2)}, u32[]{:S(2)}) collective-permute-start(bf16[512,1024]{1,0:T(8,128)(2,1)} %copy-done.26), channel_id=1, source_target_pairs={{8,16},{16,8},{9,17},{17,9},{10,18},{18,10},{11,19},{19,11},{12,20... | collective-permute-start | bytes 3145736 | tf_op jit(solution)/shard_map/ppermute | solution.py:80
  127.1 86.0 %collective-permute-start.45 = (bf16[1024,512]{1,0:T(8,128)(2,1)}, bf16[1024,512]{1,0:T(8,128)(2,1)}, u32[]{:S(2)}, u32[]{:S(2)}) collective-permute-start(bf16[1024,512]{1,0:T(8,128)(2,1)} %shard_map.98.refs_8_), channel_id=1, source_target_pairs={{0,1},{1,0},{2,3},{3,2},{4,5},{5,4},{6,7},{7,6},{8,9},{9,8},{10,11... | collective-permute-start | bytes 3145736 | tf_op jit(solution)/shard_map/ppermute | solution.py:15
  129.4 83.7 %collective-permute-start.44 = (bf16[512,1024]{1,0:T(8,128)(2,1)}, bf16[512,1024]{1,0:T(8,128)(2,1)}, u32[]{:S(2)}, u32[]{:S(2)}) collective-permute-start(bf16[512,1024]{1,0:T(8,128)(2,1)} %shard_map.97.refs_6_), channel_id=1, source_target_pairs={{0,1},{1,0},{2,3},{3,2},{4,5},{5,4},{6,7},{7,6},{8,9},{9,8},{10,11... | collective-permute-start | bytes 3145736 | tf_op jit(solution)/shard_map/ppermute | solution.py:15
  134.2 58.2 %collective-permute-start.37 = (f32[4,96,128]{1,2,0:T(8,128)}, f32[4,96,128]{1,2,0:T(8,128)}, u32[]{:S(2)}, u32[]{:S(2)}) collective-permute-start(f32[4,96,128]{1,2,0:T(8,128)} %copy.37), channel_id=1, source_target_pairs={{0,1},{1,0},{2,3},{3,2},{4,5},{5,4},{6,7},{7,6},{8,9},{9,8},{10,11... | collective-permute-start | bytes 589832 | tf_op jit(solution)/shard_map/ppermute | solution.py:15
  139.9 38.3 %collective-permute-start.33 = (bf16[1,32,1024]{2,1,0:T(8,128)(2,1)S(1)}, bf16[1,32,1024]{2,1,0:T(8,128)(2,1)S(1)}, u32[]{:S(2)}, u32[]{:S(2)}) collective-permute-start(bf16[1,32,1024]{2,1,0:T(8,128)(2,1)S(1)} %get-tuple-element.158), channel_id=1, source_target_pairs={{0,6},{1,7},{2,4},{3,5},{4,2},{5,3},{6,0},{7,1},{8,14},{9,15},{10,... | collective-permute-start | bytes 196616 | tf_op jit(solution)/shard_map/ppermute | solution.py:15
  141.9 59.8 %collective-permute-start.38 = (bf16[64,1024]{1,0:T(8,128)(2,1)}, bf16[64,1024]{1,0:T(8,128)(2,1)}, u32[]{:S(2)}, u32[]{:S(2)}) collective-permute-start(bf16[64,1024]{1,0:T(8,128)(2,1)} %pad_maximum_fusion.8), channel_id=1, source_target_pairs={{0,24},{8,16},{16,8},{1,25},{9,17},{17,9},{2,26},{10,18},{18,10},{... | collective-permute-start | bytes 393224 | tf_op jit(solution)/shard_map/ppermute | solution.py:348
  178.8 23.0 %collective-permute-start.39 = (bf16[64,1024]{1,0:T(8,128)(2,1)}, bf16[64,1024]{1,0:T(8,128)(2,1)}, u32[]{:S(2)}, u32[]{:S(2)}) collective-permute-start(bf16[64,1024]{1,0:T(8,128)(2,1)} %pad_maximum_fusion.8), channel_id=1, source_target_pairs={{0,16},{8,24},{1,17},{9,25},{2,18},{10,26},{3,19},{11,27},{4,20},{... | collective-permute-start | bytes 393224 | tf_op jit(solution)/shard_map/ppermute | solution.py:348
  201.8 36.3 %collective-permute-start.52 = (bf16[512,1024]{1,0:T(8,128)(2,1)}, bf16[512,1024]{1,0:T(8,128)(2,1)}, u32[]{:S(2)}, u32[]{:S(2)}) collective-permute-start(bf16[512,1024]{1,0:T(8,128)(2,1)} %shard_map.101.refs_6_), channel_id=1, source_target_pairs={{0,1},{1,0},{2,3},{3,2},{4,5},{5,4},{6,7},{7,6},{8,9},{9,8},{10,11... | collective-permute-start | bytes 3145736 | tf_op jit(solution)/shard_map/ppermute | solution.py:15
  (89 other events, 908.3 us)

commit v4 on v2

--- a/solution.py
+++ b/solution.py
@@ -87,14 +87,22 @@
 
 
 def choose_body(which, *refs):
-    *sources, target, sem = refs
+    *sources, target, sems = refs
+    rows = target.shape[0] // 4
     for place, source in enumerate(sources):
 
         @pl.when(which[0] == place)
         def _():
-            copy = pltpu.make_async_copy(source, target, sem)
-            copy.start()
-            copy.wait()
+            copies = [
+                pltpu.make_async_copy(
+                    source.at[pl.ds(k * rows, rows)], target.at[pl.ds(k * rows, rows)], sems.at[k]
+                )
+                for k in range(4)
+            ]
+            for copy in copies:
+                copy.start()
+            for copy in copies:
+                copy.wait()
 
 
 def choose(values, layer, section, sections):
@@ -108,7 +116,7 @@
         out_shape=jax.ShapeDtypeStruct(value.shape, value.dtype),
         in_specs=[pl.BlockSpec(memory_space=pltpu.SMEM)] + [pl.BlockSpec(memory_space=pl.ANY)] * len(keys),
         out_specs=pl.BlockSpec(memory_space=pltpu.VMEM),
-        scratch_shapes=[pltpu.SemaphoreType.DMA],
+        scratch_shapes=[pltpu.SemaphoreType.DMA((4,))],
         cost_estimate=pl.CostEstimate(flops=0, bytes_accessed=2 * value.size * 2, transcendentals=0),
     )(which.reshape(1), *[values[key] for key in keys])
 
@@ -171,6 +179,32 @@
         term = dot_t(moved.astype(BF16), after_value[...])
         total = term if total is None else total + term
     part[...] = total.astype(part.dtype)
+
+
+def value_step(terms, hidden):
+    rows, kv = terms[0].shape
+    width = hidden.shape[1]
+
+    def body(*refs):
+        *parts, rows_in, out = refs
+        wide = rows_in[...].astype(F32)
+        inverse = lax.rsqrt(jnp.sum(wide * wide, axis=1, keepdims=True) / width + EPSILON)
+        total = parts[0][...].astype(F32)
+        for part in parts[1:]:
+            total = total + part[...].astype(F32)
+        out[:, :kv] = (total * inverse).astype(BF16)
+        high = inverse.astype(BF16).astype(F32)
+        lane = lax.broadcasted_iota(jnp.int32, (rows, 128), 1)
+        out[:, kv:] = jnp.where(lane < 64, high, inverse - high).astype(BF16)
+
+    return pl.pallas_call(
+        body,
+        out_shape=jax.ShapeDtypeStruct((rows, kv + 128), BF16),
+        compiler_params=PARAMS,
+        cost_estimate=pl.CostEstimate(
+            flops=4 * rows * width, bytes_accessed=2 * rows * (width + 5 * kv), transcendentals=rows
+        ),
+    )(*terms, hidden)
 
 
 def layer_step(pieces, state, hidden, value_near, value_far, next_near, next_far, part_dtype):
@@ -278,22 +312,9 @@
     output_from, state = lax.optimization_barrier((output_from, state))
     value_from = {0: value_scaled, **exchange(value_scaled, near, sections)}
     value_sum_terms, value_from = lax.optimization_barrier((value_sum_terms, value_from))
-    value_sum = sum(term.astype(F32) for term in value_sum_terms)
-    hidden_f32 = hidden.astype(F32)
-    inverse = lax.rsqrt(jnp.mean(hidden_f32 * hidden_f32, axis=-1, keepdims=True) + EPSILON)
-    value_act = (value_sum * inverse).astype(BF16)
-    value_low = jnp.dot(value_act, value_proj[0], preferred_element_type=F32)
+    value_rows = value_step(value_sum_terms, hidden)
+    value_low = jnp.dot(value_rows[:, :kv], value_proj[0], preferred_element_type=F32)
     grad_low_top = jnp.dot(cotangent, grad_proj[0], preferred_element_type=F32)
-    inverse_high = inverse.astype(BF16)
-    inverse_low = (inverse - inverse_high.astype(F32)).astype(BF16)
-    value_rows = jnp.concatenate(
-        [
-            value_act,
-            jnp.broadcast_to(inverse_high, (tokens, 64)),
-            jnp.broadcast_to(inverse_low, (tokens, 64)),
-        ],
-        axis=1,
-    )
 
     value_rows, own_output = lax.optimization_barrier((value_rows, output_weight[0]))
     value_rows_from = to_groups(jnp.pad(value_rows, ((0, padded - tokens), (0, 0))), 0)

time: 251 us -> 253 us (level)
  waiting for transfers between devices: 70.3 us -> 78.8 us
  starting transfers between devices: 101 us -> 97.6 us
    ppermute x3, waiting for transfers between devices: 24 us -> 30.3 us  [per_device(): message_from.append(lax.ppermute(message(section ^ step), 'section', pairs))]
  transfers between devices with their start and end apart: 60 -> 60, of which waited for: 27 -> 26; matrix products, arithmetic and copies ran while one was open for 14% -> 12% of each run, Pallas kernels for 9% -> 9%
where the time goes in v4:
time: 253 us; the launch traced here: 252 us
  starting transfers between devices  97.6 us (39%)
  waiting for transfers between devices  78.8 us (31%)
  Pallas kernels  24.8 us (10%)
  local copies, waits for them, and re-layouts  23.3 us (9%)
  matrix products  13.3 us (5%)
  other arithmetic  13.2 us (5%)
    ppermute x48, starting transfers between devices, swap(): lax.ppermute(value, axis, [(i, i ^ step) for i in range(lax.axis_size(axi...  64.4 us
    ppermute x48, waiting for transfers between devices, swap(): lax.ppermute(value, axis, [(i, i ^ step) for i in range(lax.axis_size(axi...  48.5 us
    ppermute x3, waiting for transfers between devices, per_device(): message_from.append(lax.ppermute(message(section ^ step), 'section', pairs))  30.3 us
    ppermute x3, starting transfers between devices, per_device(): message_from.append(lax.ppermute(message(section ^ step), 'section', pairs))  21 us
    pallas_call x6, Pallas kernels, choose(): pl.pallas_call(choose_body, out_shape=jax.ShapeDtypeStruct(value.shape, v...  13.5 us
    unnamed x93, local copies, waits for them, and re-layouts  12.9 us
    ppermute x6, starting transfers between devices, exchange(): lax.ppermute(value, 'section', [(i, i ^ step) for i in range(1, sections)...  10.1 us
    pallas_call x3, Pallas kernels, layer_step(): pl.pallas_call(lambda *refs: layer_body(False, *refs), out_shape=(jax.Sha...  9.15 us
  transfers between devices with their start and end apart: 60, of which 26 were waited for; matrix products, arithmetic and copies ran while one was open for 12% of the time, Pallas kernels for 9%

profile of v4, /device:TPU:0, one launch (start us, length us, event | category | flops | bytes accessed | tf_op | source)
XLA Modules:
  0.0 252.0 jit_solution(11394688862246798002)
XLA Ops:
  6.4 5.1 %collective-permute-start.4 = (bf16[1,1,32,1024]{3,2,1,0:T(8,128)(2,1)S(1)}, bf16[1,1,32,1024]{3,2,1,0:T(8,128)(2,1)S(1)}, u32[]{:S(2)}, u32[]{:S(2)}) collective-permute-start(bf16[1,1,32,1024]{3,2,1,0:T(8,128)(2,1)S(1)} %slice_bitcast_fusion.10), channel_id=1, source_target_pairs={{0,6},{1,7},{2,4},{3,5},{4,2},{5,3},{6,0},{7,1},{8,14},{9,15},{10,... | collective-permute-start | bytes 196616 | tf_op jit(solution)/shard_map/ppermute | solution.py:15
  15.8 2.8 %collective-permute-start.11 = (bf16[1,1,96,1024]{3,2,1,0:T(8,128)(2,1)S(1)}, bf16[1,1,96,1024]{3,2,1,0:T(8,128)(2,1)S(1)}, u32[]{:S(2)}, u32[]{:S(2)}) collective-permute-start(bf16[1,1,96,1024]{3,2,1,0:T(8,128)(2,1)S(1)} %get-tuple-element.95), channel_id=1, source_target_pairs={{0,6},{1,7},{2,4},{3,5},{4,2},{5,3},{6,0},{7,1},{8,14},{9,15},{10,... | collective-permute-start | bytes 589832 | tf_op jit(solution)/shard_map/ppermute | solution.py:15
  19.3 6.9 %collective-permute-done.2 = bf16[1,1,32,1024]{3,2,1,0:T(8,128)(2,1)S(1)} collective-permute-done((bf16[1,1,32,1024]{3,2,1,0:T(8,128)(2,1)S(1)}, bf16[1,1,32,1024]{3,2,1,0:T(8,128)(2,1)S(1)}, u32[]{:S(2)}, u32[]{:S(2)}) %collective-permute-start.2) | collective-permute-done | bytes 65568 | tf_op jit(solution)/shard_map/ppermute | solution.py:15
  30.1 8.1 %collective-permute-done.10 = bf16[1,1,96,1024]{3,2,1,0:T(8,128)(2,1)} collective-permute-done((bf16[1,1,96,1024]{3,2,1,0:T(8,128)(2,1)}, bf16[1,1,96,1024]{3,2,1,0:T(8,128)(2,1)}, u32[]{:S(2)}, u32[]{:S(2)}) %collective-permute-start.10) | collective-permute-done | bytes 196640 | tf_op jit(solution)/shard_map/ppermute | solution.py:15
  44.6 2.9 %fusion.7 = f32[384,1024]{1,0:T(8,128)} fusion(bf16[512,1024]{1,0:T(8,128)(2,1)} %fusion.refs_0_, bf16[384,1024]{1,0:T(8,128)(2,1)S(1)} %bitcast.184), kind=kOutput, calls=%fused_computation.17 | convolution fusion | flops 402653184 | bytes 3014656 | tf_op jit(solution)/shard_map/dot_general | solution.py:309
  49.9 2.4 add_convert_fusion
  52.4 2.3 collective-permute-start.15
  57.9 16.9 %collective-permute-start.23 = (bf16[192,1024]{1,0:T(8,128)(2,1)S(1)}, bf16[192,1024]{1,0:T(8,128)(2,1)S(1)}, u32[]{:S(2)}, u32[]{:S(2)}) collective-permute-start(bf16[192,1024]{1,0:T(8,128)(2,1)S(1)} %get-tuple-element.145), channel_id=1, source_target_pairs={{0,24},{8,16},{16,8},{1,25},{9,17},{17,9},{2,26},{10,18},{18,10},{... | collective-permute-start | bytes 1179656 | tf_op jit(solution)/shard_map/ppermute | solution.py:306
  74.8 2.8 %collective-permute-start.21 = (bf16[192,1024]{1,0:T(8,128)(2,1)S(1)}, bf16[192,1024]{1,0:T(8,128)(2,1)S(1)}, u32[]{:S(2)}, u32[]{:S(2)}) collective-permute-start(bf16[192,1024]{1,0:T(8,128)(2,1)S(1)} %get-tuple-element.146), channel_id=1, source_target_pairs={{0,8},{16,24},{24,16},{1,9},{17,25},{25,17},{2,10},{18,26},{26,18}... | collective-permute-start | bytes 1179656 | tf_op jit(solution)/shard_map/ppermute | solution.py:306
  85.0 5.5 %collective-permute-done.21 = bf16[192,1024]{1,0:T(8,128)(2,1)S(1)} collective-permute-done((bf16[192,1024]{1,0:T(8,128)(2,1)S(1)}, bf16[192,1024]{1,0:T(8,128)(2,1)S(1)}, u32[]{:S(2)}, u32[]{:S(2)}) %collective-permute-start.21) | collective-permute-done | bytes 393248 | tf_op jit(solution)/shard_map/ppermute | solution.py:306
  91.9 23.3 %collective-permute-done.22 = bf16[192,1024]{1,0:T(8,128)(2,1)S(1)} collective-permute-done((bf16[192,1024]{1,0:T(8,128)(2,1)S(1)}, bf16[192,1024]{1,0:T(8,128)(2,1)S(1)}, u32[]{:S(2)}, u32[]{:S(2)}) %collective-permute-start.22) | collective-permute-done | bytes 393248 | tf_op jit(solution)/shard_map/ppermute | solution.py:306
  119.7 2.4 collective-permute-done.8
  135.9 3.7 %collective-permute-done.35 = f32[96,128]{0,1:T(8,128)S(1)} collective-permute-done((f32[96,128]{0,1:T(8,128)S(1)}, f32[96,128]{0,1:T(8,128)S(1)}, u32[]{:S(2)}, u32[]{:S(2)}) %collective-permute-start.35) | collective-permute-done | bytes 49184 | tf_op jit(solution)/shard_map/ppermute | solution.py:15
  146.9 2.3 shard_map.98.refs_6_
  155.0 3.1 %shard_map.96 = (f32[128,1024]{1,0:T(8,128)S(1)}, bf16[128,1024]{1,0:T(8,128)(2,1)S(1)}) custom-call(bf16[32,1152]{1,0:T(8,128)(2,1)S(1)} %shard_map.93.refs_0_, bf16[32,1152]{1,0:T(8,128)(2,1)S(1)} %collective-permute-done.24.refs_1_, bf16[32,1152]{1,0:T(8,128)(2,1)S(1)} %collective-permute-done.25.refs_2_, ...), custom_call_target="tpu_custom_call" | custom-call | flops 536870912 | bytes 5767168 | tf_op jit(solution)/shard_map/pallas_call | solution.py:214
  168.3 2.9 %collective-permute-done.31 = bf16[1,32,1024]{2,1,0:T(8,128)(2,1)S(1)} collective-permute-done((bf16[1,32,1024]{2,1,0:T(8,128)(2,1)S(1)}, bf16[1,32,1024]{2,1,0:T(8,128)(2,1)S(1)}, u32[]{:S(2)}, u32[]{:S(2)}) %collective-permute-start.31) | collective-permute-done | bytes 65568 | tf_op jit(solution)/shard_map/ppermute | solution.py:15
  173.5 2.5 collective-permute-start.37
  180.5 3.1 %shard_map.100 = (f32[128,1024]{1,0:T(8,128)S(1)}, bf16[128,1024]{1,0:T(8,128)(2,1)S(1)}) custom-call(bf16[32,1152]{1,0:T(8,128)(2,1)S(1)} %shard_map.97.refs_0_, bf16[32,1152]{1,0:T(8,128)(2,1)S(1)} %collective-permute-done.37.refs_1_, bf16[32,1152]{1,0:T(8,128)(2,1)S(1)} %collective-permute-done.38.refs_2_, ...), custom_call_target="tpu_custom_call" | custom-call | flops 536870912 | bytes 5767168 | tf_op jit(solution)/shard_map/pallas_call | solution.py:214
  187.1 2.4 collective-permute-start.43
  198.7 2.5 collective-permute-start.46
  208.8 3.0 %shard_map.103 = (f32[128,1024]{1,0:T(8,128)}, f32[128,64]{1,0:T(8,128)S(1)}) custom-call(bf16[32,1152]{1,0:T(8,128)(2,1)S(1)} %shard_map.101.refs_0_, bf16[32,1152]{1,0:T(8,128)(2,1)} %collective-permute-done.46.refs_1_, bf16[32,1152]{1,0:T(8,128)(2,1)} %collective-permute-done.47.refs_2_, bf16[32,1152]{1,0:T(8,128)(2,1)S(1)} %collective-permute-done.48.refs_3_, ...), custom_call_target="tpu_custom_call" | custom-call | flops 285212672 | bytes 3801088 | tf_op jit(solution)/shard_map/pallas_call | solution.py:214
  218.2 2.3 collective-permute-done.52
  225.9 7.6 %collective-permute-start.56 = (bf16[8,32,64]{1,2,0:T(8,128)(2,1)}, bf16[8,32,64]{1,2,0:T(8,128)(2,1)S(1)}, u32[]{:S(2)}, u32[]{:S(2)}) collective-permute-start(bf16[8,32,64]{1,2,0:T(8,128)(2,1)} %get-tuple-element.83), channel_id=1, source_target_pairs={{0,8},{8,0},{16,24},{24,16},{1,9},{9,1},{17,25},{25,17},{2,10},{10... | collective-permute-start | bytes 98312 | tf_op jit(solution)/shard_map/ppermute | solution.py:15
  237.7 3.3 %collective-permute-done.55 = bf16[8,32,64]{1,2,0:T(8,128)(2,1)S(1)} collective-permute-done((bf16[8,32,64]{1,2,0:T(8,128)(2,1)}, bf16[8,32,64]{1,2,0:T(8,128)(2,1)S(1)}, u32[]{:S(2)}, u32[]{:S(2)}) %collective-permute-start.55) | collective-permute-done | bytes 32800 | tf_op jit(solution)/shard_map/ppermute | solution.py:15
  (266 shorter events, 130.9 us)
Async XLA Ops:
  0.0 47.6 %collective-permute-start.1 = (bf16[1024,512]{1,0:T(8,128)(2,1)}, bf16[1024,512]{1,0:T(8,128)(2,1)}, u32[]{:S(2)}, u32[]{:S(2)}) collective-permute-start(bf16[1024,512]{1,0:T(8,128)(2,1)} %bitcast.refs_0_), channel_id=1, source_target_pairs={{8,24},{24,8},{9,25},{25,9},{10,26},{26,10},{11,27},{27,11},{12,28... | collective-permute-start | bytes 3145736 | tf_op jit(solution)/shard_map/ppermute | solution.py:80
  1.8 45.8 %collective-permute-start = (bf16[1024,512]{1,0:T(8,128)(2,1)}, bf16[1024,512]{1,0:T(8,128)(2,1)}, u32[]{:S(2)}, u32[]{:S(2)}) collective-permute-start(bf16[1024,512]{1,0:T(8,128)(2,1)} %bitcast.refs_0_), channel_id=1, source_target_pairs={{16,24},{24,16},{17,25},{25,17},{18,26},{26,18},{19,27},{27,19},{2... | collective-permute-start | bytes 3145736 | tf_op jit(solution)/shard_map/ppermute | solution.py:80
  14.0 35.9 %collective-permute-start.12 = (bf16[512,1024]{1,0:T(8,128)(2,1)}, bf16[512,1024]{1,0:T(8,128)(2,1)}, u32[]{:S(2)}, u32[]{:S(2)}) collective-permute-start(bf16[512,1024]{1,0:T(8,128)(2,1)} %fusion.refs_0_), channel_id=1, source_target_pairs={{0,1},{1,0},{2,3},{3,2},{4,5},{5,4},{6,7},{7,6},{8,9},{9,8},{10,11... | collective-permute-start | bytes 3145736 | tf_op jit(solution)/shard_map/ppermute | solution.py:15
  15.8 11.8 %collective-permute-start.11 = (bf16[1,1,96,1024]{3,2,1,0:T(8,128)(2,1)S(1)}, bf16[1,1,96,1024]{3,2,1,0:T(8,128)(2,1)S(1)}, u32[]{:S(2)}, u32[]{:S(2)}) collective-permute-start(bf16[1,1,96,1024]{3,2,1,0:T(8,128)(2,1)S(1)} %get-tuple-element.95), channel_id=1, source_target_pairs={{0,6},{1,7},{2,4},{3,5},{4,2},{5,3},{6,0},{7,1},{8,14},{9,15},{10,... | collective-permute-start | bytes 589832 | tf_op jit(solution)/shard_map/ppermute | solution.py:15
  27.5 13.3 %collective-permute-start.9 = (bf16[1,1,96,1024]{3,2,1,0:T(8,128)(2,1)}, bf16[1,1,96,1024]{3,2,1,0:T(8,128)(2,1)S(1)}, u32[]{:S(2)}, u32[]{:S(2)}) collective-permute-start(bf16[1,1,96,1024]{3,2,1,0:T(8,128)(2,1)} %get-tuple-element.97), channel_id=1, source_target_pairs={{0,2},{1,3},{2,0},{3,1},{4,6},{5,7},{6,4},{7,5},{8,10},{9,11},{10,... | collective-permute-start | bytes 589832 | tf_op jit(solution)/shard_map/ppermute | solution.py:15
  38.2 16.6 %collective-permute-start.17 = (bf16[512,1024]{1,0:T(8,128)(2,1)}, bf16[512,1024]{1,0:T(8,128)(2,1)}, u32[]{:S(2)}, u32[]{:S(2)}) collective-permute-start(bf16[512,1024]{1,0:T(8,128)(2,1)} %fusion.refs_0_), channel_id=1, source_target_pairs={{8,24},{24,8},{9,25},{25,9},{10,26},{26,10},{11,27},{27,11},{12,28... | collective-permute-start | bytes 3145736 | tf_op jit(solution)/shard_map/ppermute | solution.py:80
  40.9 17.1 %collective-permute-start.16 = (bf16[512,1024]{1,0:T(8,128)(2,1)}, bf16[512,1024]{1,0:T(8,128)(2,1)}, u32[]{:S(2)}, u32[]{:S(2)}) collective-permute-start(bf16[512,1024]{1,0:T(8,128)(2,1)} %fusion.refs_0_), channel_id=1, source_target_pairs={{16,24},{24,16},{17,25},{25,17},{18,26},{26,18},{19,27},{27,19},{2... | collective-permute-start | bytes 3145736 | tf_op jit(solution)/shard_map/ppermute | solution.py:80
  49.8 30.4 %collective-permute-start.5 = (bf16[1024,512]{1,0:T(8,128)(2,1)}, bf16[1024,512]{1,0:T(8,128)(2,1)S(1)}, u32[]{:S(2)}, u32[]{:S(2)}) collective-permute-start(bf16[1024,512]{1,0:T(8,128)(2,1)} %shard_map.91), channel_id=1, source_target_pairs={{0,1},{1,0},{2,3},{3,2},{4,5},{5,4},{6,7},{7,6},{8,9},{9,8},{10,11... | collective-permute-start | bytes 3145736 | tf_op jit(solution)/shard_map/ppermute | solution.py:15
  52.4 22.4 %collective-permute-start.15 = (bf16[1,96,1024]{2,1,0:T(8,128)(2,1)S(1)}, bf16[1,96,1024]{2,1,0:T(8,128)(2,1)S(1)}, u32[]{:S(2)}, u32[]{:S(2)}) collective-permute-start(bf16[1,96,1024]{2,1,0:T(8,128)(2,1)S(1)} %get-tuple-element.90), channel_id=1, source_target_pairs={{0,6},{1,7},{2,4},{3,5},{4,2},{5,3},{6,0},{7,1},{8,14},{9,15},{10,... | collective-permute-start | bytes 589832 | tf_op jit(solution)/shard_map/ppermute | solution.py:15
  54.8 22.9 %collective-permute-start.14 = (bf16[1,96,1024]{2,1,0:T(8,128)(2,1)S(1)}, bf16[1,96,1024]{2,1,0:T(8,128)(2,1)S(1)}, u32[]{:S(2)}, u32[]{:S(2)}) collective-permute-start(bf16[1,96,1024]{2,1,0:T(8,128)(2,1)S(1)} %get-tuple-element.91), channel_id=1, source_target_pairs={{0,4},{1,5},{2,6},{3,7},{4,0},{5,1},{6,2},{7,3},{8,12},{9,13},{10,... | collective-permute-start | bytes 589832 | tf_op jit(solution)/shard_map/ppermute | solution.py:15
  54.8 24.2 %collective-permute-start.13 = (bf16[1,96,1024]{2,1,0:T(8,128)(2,1)S(1)}, bf16[1,96,1024]{2,1,0:T(8,128)(2,1)S(1)}, u32[]{:S(2)}, u32[]{:S(2)}) collective-permute-start(bf16[1,96,1024]{2,1,0:T(8,128)(2,1)S(1)} %get-tuple-element.92), channel_id=1, source_target_pairs={{0,2},{1,3},{2,0},{3,1},{4,6},{5,7},{6,4},{7,5},{8,10},{9,11},{10,... | collective-permute-start | bytes 589832 | tf_op jit(solution)/shard_map/ppermute | solution.py:15
  57.9 26.4 %collective-permute-start.23 = (bf16[192,1024]{1,0:T(8,128)(2,1)S(1)}, bf16[192,1024]{1,0:T(8,128)(2,1)S(1)}, u32[]{:S(2)}, u32[]{:S(2)}) collective-permute-start(bf16[192,1024]{1,0:T(8,128)(2,1)S(1)} %get-tuple-element.145), channel_id=1, source_target_pairs={{0,24},{8,16},{16,8},{1,25},{9,17},{17,9},{2,26},{10,18},{18,10},{... | collective-permute-start | bytes 1179656 | tf_op jit(solution)/shard_map/ppermute | solution.py:306
  74.8 15.7 %collective-permute-start.21 = (bf16[192,1024]{1,0:T(8,128)(2,1)S(1)}, bf16[192,1024]{1,0:T(8,128)(2,1)S(1)}, u32[]{:S(2)}, u32[]{:S(2)}) collective-permute-start(bf16[192,1024]{1,0:T(8,128)(2,1)S(1)} %get-tuple-element.146), channel_id=1, source_target_pairs={{0,8},{16,24},{24,16},{1,9},{17,25},{25,17},{2,10},{18,26},{26,18}... | collective-permute-start | bytes 1179656 | tf_op jit(solution)/shard_map/ppermute | solution.py:306
  77.7 37.6 %collective-permute-start.22 = (bf16[192,1024]{1,0:T(8,128)(2,1)S(1)}, bf16[192,1024]{1,0:T(8,128)(2,1)S(1)}, u32[]{:S(2)}, u32[]{:S(2)}) collective-permute-start(bf16[192,1024]{1,0:T(8,128)(2,1)S(1)} %get-tuple-element.147), channel_id=1, source_target_pairs={{0,16},{8,24},{24,8},{1,17},{9,25},{25,9},{2,18},{10,26},{26,10},{... | collective-permute-start | bytes 1179656 | tf_op jit(solution)/shard_map/ppermute | solution.py:306
  79.4 38.1 %collective-permute-start.20 = (bf16[32,1152]{1,0:T(8,128)(2,1)S(1)}, bf16[32,1152]{1,0:T(8,128)(2,1)S(1)}, u32[]{:S(2)}, u32[]{:S(2)}) collective-permute-start(bf16[32,1152]{1,0:T(8,128)(2,1)S(1)} %get-tuple-element.138), channel_id=1, source_target_pairs={{8,16},{16,8},{9,17},{17,9},{10,18},{18,10},{11,19},{19,11},{12,20... | collective-permute-start | bytes 221192 | tf_op jit(solution)/shard_map/ppermute | solution.py:294
  80.2 49.5 %collective-permute-start.28 = (bf16[1024,512]{1,0:T(8,128)(2,1)}, bf16[1024,512]{1,0:T(8,128)(2,1)}, u32[]{:S(2)}, u32[]{:S(2)}) collective-permute-start(bf16[1024,512]{1,0:T(8,128)(2,1)} %bitcast.refs_0_), channel_id=1, source_target_pairs={{8,16},{16,8},{9,17},{17,9},{10,18},{18,10},{11,19},{19,11},{12,20... | collective-permute-start | bytes 3145736 | tf_op jit(solution)/shard_map/ppermute | solution.py:80
  84.4 33.2 %collective-permute-start.19 = (bf16[32,1152]{1,0:T(8,128)(2,1)S(1)}, bf16[32,1152]{1,0:T(8,128)(2,1)S(1)}, u32[]{:S(2)}, u32[]{:S(2)}) collective-permute-start(bf16[32,1152]{1,0:T(8,128)(2,1)S(1)} %get-tuple-element.139), channel_id=1, source_target_pairs={{8,24},{24,8},{9,25},{25,9},{10,26},{26,10},{11,27},{27,11},{12,28... | collective-permute-start | bytes 221192 | tf_op jit(solution)/shard_map/ppermute | solution.py:294
  90.6 29.2 %collective-permute-start.18 = (bf16[32,1152]{1,0:T(8,128)(2,1)S(1)}, bf16[32,1152]{1,0:T(8,128)(2,1)S(1)}, u32[]{:S(2)}, u32[]{:S(2)}) collective-permute-start(bf16[32,1152]{1,0:T(8,128)(2,1)S(1)} %get-tuple-element.140), channel_id=1, source_target_pairs={{16,24},{24,16},{17,25},{25,17},{18,26},{26,18},{19,27},{27,19},{2... | collective-permute-start | bytes 221192 | tf_op jit(solution)/shard_map/ppermute | solution.py:294
  124.2 21.5 %collective-permute-start.40 = (bf16[512,1024]{1,0:T(8,128)(2,1)}, bf16[512,1024]{1,0:T(8,128)(2,1)}, u32[]{:S(2)}, u32[]{:S(2)}) collective-permute-start(bf16[512,1024]{1,0:T(8,128)(2,1)} %fusion.refs_0_), channel_id=1, source_target_pairs={{8,16},{16,8},{9,17},{17,9},{10,18},{18,10},{11,19},{19,11},{12,20... | collective-permute-start | bytes 3145736 | tf_op jit(solution)/shard_map/ppermute | solution.py:80
  129.7 24.3 %collective-permute-start.27 = (bf16[512,1024]{1,0:T(8,128)(2,1)}, bf16[512,1024]{1,0:T(8,128)(2,1)}, u32[]{:S(2)}, u32[]{:S(2)}) collective-permute-start(bf16[512,1024]{1,0:T(8,128)(2,1)} %shard_map.94.refs_6_), channel_id=1, source_target_pairs={{0,1},{1,0},{2,3},{3,2},{4,5},{5,4},{6,7},{7,6},{8,9},{9,8},{10,11... | collective-permute-start | bytes 3145736 | tf_op jit(solution)/shard_map/ppermute | solution.py:15
  132.1 21.9 %collective-permute-start.29 = (bf16[1024,512]{1,0:T(8,128)(2,1)}, bf16[1024,512]{1,0:T(8,128)(2,1)}, u32[]{:S(2)}, u32[]{:S(2)}) collective-permute-start(bf16[1024,512]{1,0:T(8,128)(2,1)} %shard_map.95.refs_8_), channel_id=1, source_target_pairs={{0,1},{1,0},{2,3},{3,2},{4,5},{5,4},{6,7},{7,6},{8,9},{9,8},{10,11... | collective-permute-start | bytes 3145736 | tf_op jit(solution)/shard_map/ppermute | solution.py:15
  145.8 27.7 %collective-permute-start.42 = (bf16[1024,512]{1,0:T(8,128)(2,1)}, bf16[1024,512]{1,0:T(8,128)(2,1)}, u32[]{:S(2)}, u32[]{:S(2)}) collective-permute-start(bf16[1024,512]{1,0:T(8,128)(2,1)} %shard_map.99.refs_8_), channel_id=1, source_target_pairs={{0,1},{1,0},{2,3},{3,2},{4,5},{5,4},{6,7},{7,6},{8,9},{9,8},{10,11... | collective-permute-start | bytes 3145736 | tf_op jit(solution)/shard_map/ppermute | solution.py:15
  151.6 28.8 %collective-permute-start.41 = (bf16[512,1024]{1,0:T(8,128)(2,1)}, bf16[512,1024]{1,0:T(8,128)(2,1)}, u32[]{:S(2)}, u32[]{:S(2)}) collective-permute-start(bf16[512,1024]{1,0:T(8,128)(2,1)} %shard_map.98.refs_6_), channel_id=1, source_target_pairs={{0,1},{1,0},{2,3},{3,2},{4,5},{5,4},{6,7},{7,6},{8,9},{9,8},{10,11... | collective-permute-start | bytes 3145736 | tf_op jit(solution)/shard_map/ppermute | solution.py:15
  164.3 40.2 %collective-permute-start.49 = (bf16[512,1024]{1,0:T(8,128)(2,1)}, bf16[512,1024]{1,0:T(8,128)(2,1)}, u32[]{:S(2)}, u32[]{:S(2)}) collective-permute-start(bf16[512,1024]{1,0:T(8,128)(2,1)} %shard_map.102.refs_6_), channel_id=1, source_target_pairs={{0,1},{1,0},{2,3},{3,2},{4,5},{5,4},{6,7},{7,6},{8,9},{9,8},{10,11... | collective-permute-start | bytes 3145736 | tf_op jit(solution)/shard_map/ppermute | solution.py:15
  (81 other events, 861.1 us)
